TPU v7x, 512 devices: a whole 4x8x8 slice. The times are simulated.
512 devices in a mesh: expert: 64 (over x, z, core), replica: 8 (over y).
Axes of the slice: x: 4, y: 8, z: 8, core: 2. Of those that a mesh axis runs over, the one named last changes fastest.
Arguments:
- tokens: bfloat16 [65536, 2048], P(('expert', 'replica')), may hold values from -6 to 6
- gate_weight: bfloat16 [64, 2048, 768], P('expert', 'replica'), may hold values from -0.125 to 0.125
- up_weight: bfloat16 [64, 2048, 768], P('expert', 'replica'), may hold values from -0.125 to 0.125
- down_weight: bfloat16 [64, 768, 2048], P('expert', 'replica'), may hold values from -0.21875 to 0.21875
- value_weight: float32 [2048], replicated, may hold values from -1 to 1
- routes: int32 [65536, 1], P(('expert', 'replica')), may hold values from 0 to 63; in each aligned block of 128 rows (0 to 127, 128 to 255, ...) at most 4 rows name the same one
- gates: float32 [65536, 1], P(('expert', 'replica')), may hold values from 0.2 to 1
- node_ids: int32 [512, 128], P(('expert', 'replica')), may hold values from 0 to 15, never falling along the last dimension, each value on 1 to 16 neighbouring positions
- lambda_targets: float32 [512, 16], P(('expert', 'replica')), may hold values from -12 to 12
- above_grad: bfloat16 [65536, 2048], P(('expert', 'replica')), may hold values from -6 to 6
Outputs:
- token_grad: bfloat16 [65536, 2048], P(('expert', 'replica'))
- gate_grad: float32 [65536, 1], P(('expert', 'replica'))
- down_grad: float32 [64, 768, 2048], P('expert', 'replica')
- node_values: float32 [512, 16], P(('expert', 'replica'))
Inputs may be any that keep to these rules, and one draw needn't show every extreme that they name: In the rows of one device no expert is named by more than 4 routes, and in every draw some expert is named by exactly 4 routes of some device. `node_ids`: within each row node numbers never fall, and each of the 16 nodes holds 1 to 16 tokens, one of them exactly 16.
All inputs are finite; a program needn't handle non-finite values.
Results may differ from a plain program's by a relative error of at most 0.022.
Values may be sent and summed in bfloat16 or wider, within the bound.
No kernel may reach another device: no remote copies, remote signals or barrier semaphores. Data moves between devices by JAX's collectives and lax.ppermute only.
A program may use at most 64 MiB of HBM per device.

v0:
```python
import jax
import jax.numpy as jnp
from jax import lax
from jax.sharding import PartitionSpec as P


def local(
    tokens,
    gate_weight,
    up_weight,
    down_weight,
    value_weight,
    routes,
    gates,
    node_ids,
    lambda_targets,
    above_grad,
):
    expert_count = lax.axis_size("expert")
    local_experts = gate_weight.shape[0]
    experts = expert_count * local_experts
    tok_rows, model_width = tokens.shape
    route_width = routes.shape[1]
    route_rows = tok_rows * route_width
    capacity = 2 * route_rows // experts
    slot_total = experts * capacity
    hidden_width = gate_weight.shape[2]
    flat_routes = routes.reshape(route_rows)
    member = (flat_routes[:, None] == jnp.arange(experts, dtype=jnp.int32)[None, :]).astype(
        jnp.int32
    )
    slot_rank = jnp.sum((jnp.cumsum(member, axis=0) - member) * member, axis=1)
    slot_index = flat_routes * capacity + slot_rank
    dispatch = (jnp.arange(slot_total, dtype=jnp.int32)[:, None] == slot_index[None, :]).astype(
        jnp.bfloat16
    )
    token_routes = jnp.repeat(tokens, route_width, axis=0)
    send_rows = jnp.dot(dispatch, token_routes, preferred_element_type=jnp.float32).astype(
        jnp.bfloat16
    )
    send_rows = send_rows.reshape(expert_count, local_experts, capacity, model_width)
    gate_full, up_full, down_full = (
        lax.all_gather(gate_weight, "replica", axis=1, tiled=True),
        lax.all_gather(up_weight, "replica", axis=1, tiled=True),
        lax.all_gather(down_weight, "replica", axis=1, tiled=True),
    )
    received = lax.all_to_all(send_rows, "expert", split_axis=0, concat_axis=0, tiled=True)
    gate_act = jnp.einsum("secd,edf->secf", received, gate_full, preferred_element_type=jnp.float32)
    up_act = jnp.einsum("secd,edf->secf", received, up_full, preferred_element_type=jnp.float32)
    hidden = (jax.nn.silu(gate_act) * up_act).astype(jnp.bfloat16)
    expert_out = jnp.einsum(
        "secf,efd->secd", hidden, down_full, preferred_element_type=jnp.float32
    ).astype(jnp.bfloat16)
    gate_flat = gates.reshape(route_rows)
    returned = lax.all_to_all(expert_out, "expert", split_axis=0, concat_axis=0, tiled=True)
    route_out = jnp.dot(
        dispatch.T, returned.reshape(slot_total, model_width), preferred_element_type=jnp.float32
    )
    route_proj = jnp.sum(route_out * value_weight[None, :], axis=1)
    token_value = jnp.sum(tokens.astype(jnp.float32) * value_weight[None, :], axis=1)
    token_value = token_value + jnp.sum(
        (gate_flat * route_proj).reshape(tok_rows, route_width), axis=1
    )
    node_count = lambda_targets.shape[1]
    node_member = (
        node_ids.reshape(tok_rows)[:, None] == jnp.arange(node_count, dtype=jnp.int32)[None, :]
    ).astype(jnp.float32)
    counts = jnp.sum(node_member, axis=0)
    node_mean = jnp.sum(node_member * token_value[:, None], axis=0) / counts
    node_error = node_mean - lambda_targets[0]
    token_error = jnp.sum(node_member * node_error[None, :], axis=1)
    value_grad = (
        above_grad.astype(jnp.float32) + token_error[:, None] * value_weight[None, :]
    ).astype(jnp.bfloat16)
    grad_routes = jnp.repeat(value_grad, route_width, axis=0)
    gate_send = jnp.zeros((slot_total,), jnp.float32).at[slot_index].set(gate_flat)
    gate_send = gate_send.reshape(expert_count, local_experts, capacity)
    grad_send = jnp.dot(dispatch, grad_routes, preferred_element_type=jnp.float32).astype(
        jnp.bfloat16
    )
    grad_send = grad_send.reshape(expert_count, local_experts, capacity, model_width)
    grad_recv, gate_recv = (
        lax.all_to_all(grad_send, "expert", split_axis=0, concat_axis=0, tiled=True),
        lax.all_to_all(
            gate_send.astype(jnp.bfloat16), "expert", split_axis=0, concat_axis=0, tiled=True
        ).astype(gate_send.dtype),
    )
    out_grad = (gate_recv[..., None] * grad_recv.astype(jnp.float32)).astype(jnp.bfloat16)
    hidden_grad = jnp.einsum(
        "secd,efd->secf", out_grad, down_full, preferred_element_type=jnp.float32
    )
    sig = jax.nn.sigmoid(gate_act)
    silu_val = gate_act * sig
    slope = sig * (1.0 + gate_act * (1.0 - sig))
    gate_back = (hidden_grad * up_act * slope).astype(jnp.bfloat16)
    up_back = (hidden_grad * silu_val).astype(jnp.bfloat16)
    input_grad = (
        jnp.einsum("secf,edf->secd", gate_back, gate_full, preferred_element_type=jnp.float32)
        + jnp.einsum("secf,edf->secd", up_back, up_full, preferred_element_type=jnp.float32)
    ).astype(jnp.bfloat16)
    back_grad = lax.all_to_all(input_grad, "expert", split_axis=0, concat_axis=0, tiled=True)
    route_gate = jnp.sum(route_out * grad_routes.astype(jnp.float32), axis=1)
    route_grad = jnp.dot(
        dispatch.T, back_grad.reshape(slot_total, model_width), preferred_element_type=jnp.float32
    )
    token_grad = (
        value_grad.astype(jnp.float32)
        + jnp.sum(route_grad.reshape(tok_rows, route_width, model_width), axis=1)
    ).astype(jnp.bfloat16)
    hidden_rows = hidden.reshape(slot_total, hidden_width)
    out_rows = out_grad.reshape(slot_total, model_width)
    down_local = lax.psum_scatter(
        jnp.einsum("sf,sd->fd", hidden_rows, out_rows, preferred_element_type=jnp.float32).astype(
            jnp.bfloat16
        ),
        "replica",
        scatter_dimension=0,
        tiled=True,
    ).astype(jnp.float32)
    return (
        token_grad,
        route_gate.reshape(tok_rows, route_width),
        down_local[None],
        node_mean[None, :],
    )


def solution(mesh):
    return jax.shard_map(
        local,
        mesh=mesh,
        in_specs=(
            P(("expert", "replica"), None),
            P("expert", "replica", None),
            P("expert", "replica", None),
            P("expert", "replica", None),
            P(),
            P(("expert", "replica"), None),
            P(("expert", "replica"), None),
            P(("expert", "replica"), None),
            P(("expert", "replica"), None),
            P(("expert", "replica"), None),
        ),
        out_specs=(
            P(("expert", "replica"), None),
            P(("expert", "replica"), None),
            P("expert", "replica", None),
            P(("expert", "replica"), None),
        ),
        check_vma=False,
    )
```

profile of v0, /device:TPU:1, one launch (start us, length us, event | category | flops | bytes accessed | tf_op | source)
XLA Modules:
  0.0 315.0 jit_solution(8125932839505573424)
XLA Ops:
  11.8 1.5 convolution_convert_fusion.1
  13.7 43.2 %all_to_all.25 = bf16[64,1,4,2048]{3,2,1,0:T(4,128)(2,1)S(1)} all-to-all(bf16[64,1,4,2048]{3,2,1,0:T(4,128)(2,1)S(1)} %bitcast.119), channel_id=1, replica_groups=mesh['expert'=64,'replica'=8] {'expert'}, dimensions={0} | all-to-all | bytes 2097152 | tf_op jit(solution)/shard_map/all_to_all | solution.py:47
  56.9 5.6 %all-gather.4.cloned.1.call-done = bf16[1,2048,768]{2,1,0:T(8,128)(2,1)} async-done(((bf16[1,256,768]{2,1,0:T(8,128)(2,1)}), bf16[1,2048,768]{2,1,0:T(8,128)(2,1)}) %all-gather.4.cloned.1.call-update) | async-done | bytes 3145744 | tf_op jit(solution)/shard_map/all_gather | solution.py:43
  62.5 3.8 %fusion.28 = f32[64,1,4,768]{3,0,2,1:T(8,128)S(1)} fusion(bf16[1,2048,768]{2,1,0:T(8,128)(2,1)} %all-gather.4.cloned.1.call-done, bf16[64,1,4,2048]{3,2,1,0:T(4,128)(2,1)S(1)} %all_to_all.25), kind=kOutput, calls=%fused_computation.25 | convolution fusion | flops 805306368 | bytes 4980736 | tf_op jit(solution)/shard_map/secd,edf->secf/dot_general | solution.py:48
  66.2 44.8 %all-gather.6.cloned.1.call-done = bf16[1,2048,768]{2,1,0:T(8,128)(2,1)} async-done(((bf16[1,256,768]{2,1,0:T(8,128)(2,1)}), bf16[1,2048,768]{2,1,0:T(8,128)(2,1)}) %all-gather.6.cloned.1.call-update) | async-done | bytes 3145744 | tf_op jit(solution)/shard_map/all_gather | solution.py:44
  111.0 3.8 %fusion.31 = f32[64,1,4,768]{3,0,2,1:T(8,128)S(1)} fusion(bf16[1,2048,768]{2,1,0:T(8,128)(2,1)} %all-gather.6.cloned.1.call-done, bf16[64,1,4,2048]{3,2,1,0:T(4,128)(2,1)S(1)} %all_to_all.25), kind=kOutput, calls=%fused_computation.26 | convolution fusion | flops 805306368 | bytes 4980736 | tf_op jit(solution)/shard_map/secd,edf->secf/dot_general | solution.py:49
  115.9 43.6 %all-gather.8.cloned.1.call-done = bf16[1,768,2048]{2,1,0:T(8,128)(2,1)} async-done(((bf16[1,96,2048]{2,1,0:T(8,128)(2,1)}), bf16[1,768,2048]{2,1,0:T(8,128)(2,1)}) %all-gather.8.cloned.1.call-update) | async-done | bytes 3145744 | tf_op jit(solution)/shard_map/all_gather | solution.py:45
  159.5 2.9 fusion.21
  162.4 1.8 copy.31
  164.2 11.7 %all-to-all-start.1 = ((bf16[64,1,4,2048]{3,2,1,0:T(4,128)(2,1)}), bf16[64,1,4,2048]{3,2,1,0:T(4,128)(2,1)S(1)}, u32[]{:S(2)}, u32[]{:S(2)}) async-start(bf16[64,1,4,2048]{3,2,1,0:T(4,128)(2,1)} %copy.31), calls=%async_computation.1 | async-start | bytes 2097152 | tf_op jit(solution)/shard_map/all_to_all | solution.py:55
  177.9 26.7 %all-to-all-done.1 = bf16[64,1,4,2048]{3,2,1,0:T(4,128)(2,1)S(1)} async-done(((bf16[64,1,4,2048]{3,2,1,0:T(4,128)(2,1)}), bf16[64,1,4,2048]{3,2,1,0:T(4,128)(2,1)S(1)}, u32[]{:S(2)}, u32[]{:S(2)}) %all-to-all-start.1) | async-done | bytes 1048608 | tf_op jit(solution)/shard_map/all_to_all | solution.py:55
  204.5 6.4 %all-to-all-start.2 = ((bf16[64,1,4]{2,1,0:T(2,128)(2,1)}), bf16[64,1,4]{2,1,0:T(2,128)(2,1)}, u32[]{:S(2)}, u32[]{:S(2)}) async-start(bf16[64,1,4]{2,1,0:T(2,128)(2,1)} %convert_element_type.112), calls=%async_computation.2 | async-start | bytes 65536 | tf_op jit(solution)/shard_map/all_to_all | solution.py:84
  214.9 1.2 reshape.130
  216.1 3.8 %all-to-all-done.2 = bf16[64,1,4]{2,1,0:T(2,128)(2,1)} async-done(((bf16[64,1,4]{2,1,0:T(2,128)(2,1)}), bf16[64,1,4]{2,1,0:T(2,128)(2,1)}, u32[]{:S(2)}, u32[]{:S(2)}) %all-to-all-start.2) | async-done | bytes 544 | tf_op jit(solution)/shard_map/all_to_all | solution.py:84
  219.9 6.5 %all-to-all-start.3 = ((bf16[64,1,4,2048]{3,2,1,0:T(4,128)(2,1)}), bf16[64,1,4,2048]{3,2,1,0:T(4,128)(2,1)S(1)}, u32[]{:S(2)}, u32[]{:S(2)}) async-start(bf16[64,1,4,2048]{3,2,1,0:T(4,128)(2,1)} %bitcast.31), calls=%async_computation.3 | async-start | bytes 2097152 | tf_op jit(solution)/shard_map/all_to_all | solution.py:83
  227.3 27.7 %all-to-all-done.3 = bf16[64,1,4,2048]{3,2,1,0:T(4,128)(2,1)S(1)} async-done(((bf16[64,1,4,2048]{3,2,1,0:T(4,128)(2,1)}), bf16[64,1,4,2048]{3,2,1,0:T(4,128)(2,1)S(1)}, u32[]{:S(2)}, u32[]{:S(2)}) %all-to-all-start.3) | async-done | bytes 1048608 | tf_op jit(solution)/shard_map/all_to_all | solution.py:83
  256.5 3.5 %bitcast_convert_fusion = bf16[768,2048]{1,0:T(8,128)(2,1)} fusion(bf16[64,4,768]{2,0,1:T(8,128)(2,1)S(1)} %fusion.46, bf16[64,4,2048]{2,1,0:T(4,128)(2,1)S(1)} %fusion.38), kind=kOutput, calls=%fused_computation.1 | convolution fusion | flops 806879232 | bytes 4587520 | tf_op jit(solution)/shard_map/sf,sd->fd/dot_general | solution.py:113
  260.0 1.2 copy-done.3
  261.2 4.0 %fusion.34 = f32[64,1,4,768]{3,0,2,1:T(8,128)S(1)} fusion(bf16[1,768,2048]{2,1,0:T(8,128)(2,1)} %all-gather.8.cloned.1.call-done, bf16[64,4,2048]{2,1,0:T(4,128)(2,1)S(1)} %copy-done.3), kind=kOutput, calls=%fused_computation.27 | convolution fusion | flops 805306368 | bytes 4980736 | tf_op jit(solution)/shard_map/secd,efd->secf/dot_general | solution.py:89
  267.4 1.2 fusion.24
  268.6 1.8 copy.35
  270.4 6.2 %all-to-all-start.4 = ((bf16[64,1,4,2048]{3,2,1,0:T(4,128)(2,1)}), bf16[64,1,4,2048]{3,2,1,0:T(4,128)(2,1)S(1)}, u32[]{:S(2)}, u32[]{:S(2)}) async-start(bf16[64,1,4,2048]{3,2,1,0:T(4,128)(2,1)} %copy.35), calls=%async_computation.4 | async-start | bytes 2097152 | tf_op jit(solution)/shard_map/all_to_all | solution.py:101
  277.4 27.7 %all-to-all-done.4 = bf16[64,1,4,2048]{3,2,1,0:T(4,128)(2,1)S(1)} async-done(((bf16[64,1,4,2048]{3,2,1,0:T(4,128)(2,1)}), bf16[64,1,4,2048]{3,2,1,0:T(4,128)(2,1)S(1)}, u32[]{:S(2)}, u32[]{:S(2)}) %all-to-all-start.4) | async-done | bytes 1048608 | tf_op jit(solution)/shard_map/all_to_all | solution.py:101
  306.5 1.9 bitcast_convert_fusion.1
  (57 shorter events, 18.7 us)
Async XLA Ops:
  7.2 55.3 %all-gather.4.cloned.1.call-start = ((), (), s32[]{:S(2)}) async-start(), calls=%async_computation.6 | async-start | bytes 3538944 | tf_op jit(solution)/shard_map/all_gather | solution.py:43
  7.9 103.1 %all-gather.6.cloned.1.call-start = ((), (), s32[]{:S(2)}) async-start(), calls=%async_computation.7 | async-start | bytes 3538944 | tf_op jit(solution)/shard_map/all_gather | solution.py:44
  8.6 150.9 %all-gather.8.cloned.1.call-start = ((), (), s32[]{:S(2)}) async-start(), calls=%async_computation.8 | async-start | bytes 3538944 | tf_op jit(solution)/shard_map/all_gather | solution.py:45
  66.2 48.5 %copy-start.4 = (f32[64,1,4,768]{3,0,2,1:T(8,128)}, f32[64,1,4,768]{3,0,2,1:T(8,128)S(1)}, u32[]{:S(2)}) copy-start(f32[64,1,4,768]{3,0,2,1:T(8,128)S(1)} %fusion.28) | copy-start | bytes 2359300
  114.8 0.9 copy-start.6
  162.4 13.6 %copy-start.9 = (s32[128,1]{0,1:T(1,128)S(1)}, s32[128,1]{0,1:T(1,128)}, u32[]{:S(2)}) copy-start(s32[128,1]{0,1:T(1,128)} %param.15) | copy-start | bytes 1540
  162.4 48.8 %copy-start.1 = (bf16[128,2048]{1,0:T(8,128)(2,1)S(1)}, bf16[128,2048]{1,0:T(8,128)(2,1)}, u32[]{:S(2)}) copy-start(bf16[128,2048]{1,0:T(8,128)(2,1)} %param.10) | copy-start | bytes 1572868
  162.4 48.8 %copy-start.8 = (f32[2048]{0:T(1024)S(1)}, f32[2048]{0:T(1024)}, u32[]{:S(2)}) copy-start(f32[2048]{0:T(1024)} %param.14) | copy-start | bytes 24580
  164.2 48.9 %copy-start.10 = (f32[1,16]{1,0:T(1,128)S(1)}, f32[1,16]{1,0:T(1,128)}, u32[]{:S(2)}) copy-start(f32[1,16]{1,0:T(1,128)} %param.18) | copy-start | bytes 196
  164.2 50.2 %copy-start = (bf16[128,2048]{1,0:T(8,128)(2,1)S(1)}, bf16[128,2048]{1,0:T(8,128)(2,1)}, u32[]{:S(2)}) copy-start(bf16[128,2048]{1,0:T(8,128)(2,1)} %param.19) | copy-start | bytes 1572868
  164.2 40.3 %all-to-all-start.1 = ((bf16[64,1,4,2048]{3,2,1,0:T(4,128)(2,1)}), bf16[64,1,4,2048]{3,2,1,0:T(4,128)(2,1)S(1)}, u32[]{:S(2)}, u32[]{:S(2)}) async-start(bf16[64,1,4,2048]{3,2,1,0:T(4,128)(2,1)} %copy.31), calls=%async_computation.1 | async-start | bytes 2097152 | tf_op jit(solution)/shard_map/all_to_all | solution.py:55
  204.5 15.4 %all-to-all-start.2 = ((bf16[64,1,4]{2,1,0:T(2,128)(2,1)}), bf16[64,1,4]{2,1,0:T(2,128)(2,1)}, u32[]{:S(2)}, u32[]{:S(2)}) async-start(bf16[64,1,4]{2,1,0:T(2,128)(2,1)} %convert_element_type.112), calls=%async_computation.2 | async-start | bytes 65536 | tf_op jit(solution)/shard_map/all_to_all | solution.py:84
  219.9 35.1 %all-to-all-start.3 = ((bf16[64,1,4,2048]{3,2,1,0:T(4,128)(2,1)}), bf16[64,1,4,2048]{3,2,1,0:T(4,128)(2,1)S(1)}, u32[]{:S(2)}, u32[]{:S(2)}) async-start(bf16[64,1,4,2048]{3,2,1,0:T(4,128)(2,1)} %bitcast.31), calls=%async_computation.3 | async-start | bytes 2097152 | tf_op jit(solution)/shard_map/all_to_all | solution.py:83
  226.5 80.1 %reduce-scatter.2.cloned.1.call-start = ((), (), s32[]{:S(2)}) async-start(), calls=%async_computation.9 | async-start | bytes 3538944 | tf_op jit(solution)/shard_map/reduce_scatter | solution.py:112
  255.5 1.0 copy-start.2
  260.0 1.2 copy-start.3
  261.2 4.0 %copy-start.5 = (f32[64,1,4,768]{3,0,2,1:T(8,128)S(1)}, f32[64,1,4,768]{3,0,2,1:T(8,128)}, u32[]{:S(2)}) copy-start(f32[64,1,4,768]{3,0,2,1:T(8,128)} %copy-done.4) | copy-start | bytes 2359300
  261.2 4.0 %copy-start.12 = (bf16[1,2048,768]{2,1,0:T(8,128)(2,1)S(1)}, bf16[1,2048,768]{2,1,0:T(8,128)(2,1)}, u32[]{:S(2)}) copy-start(bf16[1,2048,768]{2,1,0:T(8,128)(2,1)} %all-gather.6.cloned.1.call-done) | copy-start | bytes 9437188
  265.3 1.1 copy-start.7
  265.3 2.1 copy-start.11
  270.4 34.8 %all-to-all-start.4 = ((bf16[64,1,4,2048]{3,2,1,0:T(4,128)(2,1)}), bf16[64,1,4,2048]{3,2,1,0:T(4,128)(2,1)S(1)}, u32[]{:S(2)}, u32[]{:S(2)}) async-start(bf16[64,1,4,2048]{3,2,1,0:T(4,128)(2,1)} %copy.35), calls=%async_computation.4 | async-start | bytes 2097152 | tf_op jit(solution)/shard_map/all_to_all | solution.py:101
Sparse Core Ops, SparseCore 0:
  10.1 52.3 all-gather.3
  64.5 46.4 all-gather.5
  113.1 46.4 all-gather.7
  260.1 40.3 reduce-scatter.1
where the time goes:
time: 316 us; the launch traced here: 315 us
  waiting for transfers between devices  182 us (58%)
  blocking collectives  43.2 us (14%)
  starting transfers between devices  31 us (10%)
  matrix products  23.7 us (8%)
  between operations  14.1 us (4%)
  local copies, waits for them, and re-layouts  11.8 us (4%)
  other arithmetic  9.39 us (3%)
    all_gather x1, waiting for transfers between devices, local(): lax.all_gather(up_weight, 'replica', axis=1, tiled=True)  44.8 us
    all_gather x1, waiting for transfers between devices, local(): lax.all_gather(down_weight, 'replica', axis=1, tiled=True)  43.6 us
    all_to_all x1, blocking collectives, local(): lax.all_to_all(send_rows, 'expert', split_axis=0, concat_axis=0, tiled=True)  43.2 us
    all_to_all x1, waiting for transfers between devices, local(): lax.all_to_all(input_grad, 'expert', split_axis=0, concat_axis=0, tiled=T...  27.7 us
    all_to_all x1, waiting for transfers between devices, local(): lax.all_to_all(grad_send, 'expert', split_axis=0, concat_axis=0, tiled=True)  27.7 us
    all_to_all x1, waiting for transfers between devices, local(): lax.all_to_all(expert_out, 'expert', split_axis=0, concat_axis=0, tiled=T...  26.7 us
    all_to_all x1, starting transfers between devices, local(): lax.all_to_all(expert_out, 'expert', split_axis=0, concat_axis=0, tiled=T...  11.7 us
    all_to_all x1, starting transfers between devices, local(): lax.all_to_all(grad_send, 'expert', split_axis=0, concat_axis=0, tiled=True)  6.53 us
  transfers between devices with their start and end apart: 8, of which 7 were waited for; matrix products, arithmetic and copies ran while one was open for 10% of the time, Pallas kernels for 0%

commit v1 on v0

v1 whole, which is shorter than its diff:
```python
import jax
import jax.numpy as jnp
from jax import lax
from jax.sharding import PartitionSpec as P

BF16 = jnp.bfloat16
F32 = jnp.float32


def exchange(rows):
    return lax.all_to_all(rows, "expert", split_axis=0, concat_axis=0, tiled=True)


def local(
    tokens,
    gate_weight,
    up_weight,
    down_weight,
    value_weight,
    routes,
    gates,
    node_ids,
    lambda_targets,
    above_grad,
):
    experts = lax.axis_size("expert")
    replicas = lax.axis_size("replica")
    tok_rows, width = tokens.shape
    hidden_width = gate_weight.shape[2]
    capacity = 2 * tok_rows // experts
    slots = experts * capacity

    expert_of = routes[:, 0]
    member = (expert_of[:, None] == jnp.arange(experts, dtype=jnp.int32)[None, :]).astype(jnp.int32)
    rank = jnp.sum((jnp.cumsum(member, axis=0) - member) * member, axis=1)
    slot_of = expert_of * capacity + rank
    both_rows = jnp.arange(2 * slots, dtype=jnp.int32)
    both_of = expert_of * (2 * capacity) + rank
    pick = jnp.concatenate([both_of, both_of + capacity])
    pick = (both_rows[:, None] == pick[None, :]).astype(BF16)
    both = jnp.dot(
        pick, jnp.concatenate([tokens, above_grad], axis=0), preferred_element_type=F32
    ).astype(BF16)

    gate_up = lax.all_gather(
        jnp.concatenate([gate_weight[0], up_weight[0]], axis=1), "replica", axis=0, tiled=True
    )
    down = lax.all_gather(down_weight[0], "replica", axis=0, tiled=True)
    head_part = jnp.sum(down_weight[0].astype(F32) * value_weight[None, :], axis=1)
    head = lax.all_to_all(
        jnp.broadcast_to(head_part[None, :], (replicas, hidden_width // replicas)),
        "replica",
        split_axis=0,
        concat_axis=0,
        tiled=True,
    ).reshape(hidden_width)

    both_in = exchange(both.reshape(experts, 2 * capacity, width))
    rows_in = both_in[:, :capacity].reshape(slots, width)
    above_in = both_in[:, capacity:].reshape(slots, width)

    acts = jnp.dot(rows_in, gate_up, preferred_element_type=F32)
    gate_act, up_act = acts[:, :hidden_width], acts[:, hidden_width:]
    sig = jax.nn.sigmoid(gate_act)
    silu = gate_act * sig
    hidden = (silu * up_act).astype(BF16)
    proj = jnp.sum(hidden.astype(F32) * head[None, :], axis=1)
    proj_back = exchange(proj.reshape(experts, capacity)).reshape(slots)

    at_slot = slot_of[:, None] == jnp.arange(slots, dtype=jnp.int32)[None, :]
    route_proj = jnp.sum(jnp.where(at_slot, proj_back[None, :], 0.0), axis=1)
    token_value = jnp.sum(tokens.astype(F32) * value_weight[None, :], axis=1)
    token_value = token_value + gates[:, 0] * route_proj
    nodes = lambda_targets.shape[1]
    in_node = node_ids[0][:, None] == jnp.arange(nodes, dtype=jnp.int32)[None, :]
    in_node = in_node.astype(F32)
    node_mean = jnp.sum(in_node * token_value[:, None], axis=0) / jnp.sum(in_node, axis=0)
    token_error = jnp.sum(in_node * (node_mean - lambda_targets[0])[None, :], axis=1)

    error_slot = jnp.sum(jnp.where(at_slot, token_error[:, None], 0.0), axis=0)
    gate_slot = jnp.sum(jnp.where(at_slot, gates, 0.0), axis=0)
    scalars = jnp.concatenate(
        [error_slot.reshape(experts, capacity), gate_slot.reshape(experts, capacity)], axis=1
    )
    scalars = exchange(scalars)
    error_in = scalars[:, :capacity].reshape(slots)
    gate_in = scalars[:, capacity:].reshape(slots)

    grad_in = (above_in.astype(F32) + error_in[:, None] * value_weight[None, :]).astype(BF16)
    out_grad = (gate_in[:, None] * grad_in.astype(F32)).astype(BF16)
    partial = lax.dot_general(
        hidden, out_grad, (((0,), (0,)), ((), ())), preferred_element_type=F32
    ).astype(BF16)
    down_grad = lax.psum_scatter(partial, "replica", scatter_dimension=0, tiled=True)

    hidden_grad = lax.dot_general(
        out_grad, down, (((1,), (1,)), ((), ())), preferred_element_type=F32
    )
    scaled = jnp.sum(hidden.astype(F32) * hidden_grad, axis=1)
    slope = sig * (1.0 + gate_act * (1.0 - sig))
    back = jnp.concatenate([hidden_grad * up_act * slope, hidden_grad * silu], axis=1).astype(BF16)
    input_grad = lax.dot_general(
        back, gate_up, (((1,), (1,)), ((), ())), preferred_element_type=F32
    ).astype(BF16)
    high = scaled.astype(BF16)
    low = (scaled - high.astype(F32)).astype(BF16)
    lane = jnp.arange(128, dtype=jnp.int32)[None, :]
    tail = jnp.where(lane == 0, high[:, None], jnp.where(lane == 1, low[:, None], 0)).astype(BF16)
    returned = jnp.concatenate([input_grad, tail], axis=1)
    returned = exchange(returned.reshape(experts, capacity, width + 128)).reshape(slots, width + 128)
    route_rows = jnp.dot(at_slot.astype(BF16), returned, preferred_element_type=F32)

    value_grad = (
        above_grad.astype(F32) + token_error[:, None] * value_weight[None, :]
    ).astype(BF16)
    token_grad = (value_grad.astype(F32) + route_rows[:, :width]).astype(BF16)
    gate_grad = (route_rows[:, width : width + 1] + route_rows[:, width + 1 : width + 2]) / gates
    return token_grad, gate_grad, down_grad.astype(F32)[None], node_mean[None, :]


def solution(mesh):
    rows = P(("expert", "replica"), None)
    weight = P("expert", "replica", None)
    return jax.shard_map(
        local,
        mesh=mesh,
        in_specs=(rows, weight, weight, weight, P(), rows, rows, rows, rows, rows),
        out_specs=(rows, rows, weight, rows),
        check_vma=False,
    )
```

time: 316 us -> 204 us (0.65)
  waiting for transfers between devices: 182 us -> 99.9 us
  blocking collectives: 43.2 us -> 0 us
  starting transfers between devices: 31 us -> 46.1 us
  matrix products: 23.7 us -> 20 us
  other arithmetic: 9.39 us -> 12.8 us
    all_gather x3 -> x2, waiting for transfers between devices: 94 us -> 0.02 us  [the longest x1 0.02 us: local(): down = lax.all_gather(down_weight[0], 'replica', axis=0, tiled=True)]
    all_to_all x1 -> x0, blocking collectives: 43.2 us -> none  [local(): lax.all_to_all(send_rows, 'expert', split_axis=0, concat_axis=0, tiled=True)]
    all_to_all x4 -> x5, starting transfers between devices: 30.9 us -> 45.8 us  [the longest x4 38.2 us: exchange(): lax.all_to_all(rows, 'expert', split_axis=0, concat_axis=0, tiled=True)]
    all_to_all x4 -> x5, waiting for transfers between devices: 85.9 us -> 99.2 us  [the longest x4 95.3 us: exchange(): lax.all_to_all(rows, 'expert', split_axis=0, concat_axis=0, tiled=True)]
    dot_general x11 -> x6, matrix products: 23.7 us -> 20 us  [the longest x1 4.9 us: local(): acts = jnp.dot(rows_in, gate_up, preferred_element_type=F32)]
  transfers between devices with their start and end apart: 8 -> 8, of which waited for: 7 -> 5; matrix products, arithmetic and copies ran while one was open for 10% -> 17% of each run, Pallas kernels for 0% -> 0%
where the time goes in v1:
time: 204 us; the launch traced here: 203 us
  waiting for transfers between devices  99.9 us (49%)
  starting transfers between devices  46.1 us (23%)
  matrix products  20 us (10%)
  between operations  14.1 us (7%)
  other arithmetic  12.8 us (6%)
  local copies, waits for them, and re-layouts  10.2 us (5%)
    all_to_all x4, waiting for transfers between devices, exchange(): lax.all_to_all(rows, 'expert', split_axis=0, concat_axis=0, tiled=True)  95.3 us
    all_to_all x4, starting transfers between devices, exchange(): lax.all_to_all(rows, 'expert', split_axis=0, concat_axis=0, tiled=True)  38.2 us
    all_to_all x1, starting transfers between devices, local(): lax.all_to_all(jnp.broadcast_to(head_part[None, :], (replicas, hidden_wid...  7.65 us
    dot_general x1, matrix products, local(): acts = jnp.dot(rows_in, gate_up, preferred_element_type=F32)  4.9 us
    dot_general x1, matrix products, local(): lax.dot_general(back, gate_up, (((1,), (1,)), ((), ())), preferred_elemen...  4.6 us
    dot_general x1, matrix products, local(): lax.dot_general(hidden, out_grad, (((0,), (0,)), ((), ())), preferred_ele...  4.34 us
  transfers between devices with their start and end apart: 8, of which 5 were waited for; matrix products, arithmetic and copies ran while one was open for 17% of the time, Pallas kernels for 0%

profile of v1, /device:TPU:1, one launch (start us, length us, event | category | flops | bytes accessed | tf_op | source)
XLA Modules:
  0.0 203.2 jit_solution(18138563093745895369)
XLA Ops:
  7.3 2.1 %pad_maximum_fusion.1 = bf16[256,1536]{1,0:T(8,128)(2,1)} fusion(bf16[256,768]{1,0:T(8,128)(2,1)} %bitcast.51, bf16[256,768]{1,0:T(8,128)(2,1)} %bitcast.52), kind=kLoop, calls=%fused_computation.21 | loop fusion | flops 1572864 | bytes 1572864 | tf_op jit(solution)/shard_map/concatenate | solution.py:46
  10.2 7.7 %all-to-all-start.1 = ((f32[8,1,96]{2,1,0:T(1,128)}), f32[8,1,96]{2,1,0:T(1,128)S(1)}, u32[]{:S(2)}, u32[]{:S(2)}) async-start(f32[8,1,96]{2,1,0:T(1,128)} %broadcast_in_dim.98), calls=%async_computation.1 | async-start | bytes 8192 | tf_op jit(solution)/shard_map/all_to_all | solution.py:50
  18.4 2.1 %fusion.2 = bf16[64,8,2048]{2,1,0:T(8,128)(2,1)} fusion(bf16[128,2048]{1,0:T(8,128)(2,1)S(1)} %copy-done.3, bf16[128,2048]{1,0:T(8,128)(2,1)S(1)} %copy-done.5, s32[256]{0:T(256)S(1)} %pad_add_fusion), kind=kOutput, calls=%fused_computation.4 | convolution fusion | flops 540147712 | bytes 3146752 | tf_op jit(solution)/shard_map/dot_general | solution.py:41
  20.5 3.8 %all-to-all-done.1 = f32[8,1,96]{2,1,0:T(1,128)S(1)} async-done(((f32[8,1,96]{2,1,0:T(1,128)}), f32[8,1,96]{2,1,0:T(1,128)S(1)}, u32[]{:S(2)}, u32[]{:S(2)}) %all-to-all-start.1) | async-done | bytes 3104 | tf_op jit(solution)/shard_map/all_to_all | solution.py:50
  24.3 15.6 %all-to-all-start = ((bf16[64,8,2048]{2,1,0:T(8,128)(2,1)}), bf16[64,8,2048]{2,1,0:T(8,128)(2,1)}, u32[]{:S(2)}, u32[]{:S(2)}) async-start(bf16[64,8,2048]{2,1,0:T(8,128)(2,1)} %fusion.2), calls=%async_computation | async-start | bytes 4194304 | tf_op jit(solution)/shard_map/all_to_all | solution.py:11
  42.0 49.1 %all-to-all-done = bf16[64,8,2048]{2,1,0:T(8,128)(2,1)} async-done(((bf16[64,8,2048]{2,1,0:T(8,128)(2,1)}), bf16[64,8,2048]{2,1,0:T(8,128)(2,1)}, u32[]{:S(2)}, u32[]{:S(2)}) %all-to-all-start) | async-done | bytes 2097184 | tf_op jit(solution)/shard_map/all_to_all | solution.py:11
  91.1 3.1 %fusion.24 = (bf16[64,4,2048]{2,1,0:T(4,128)(2,1)S(1)}, f32[64,4,2048]{2,1,0:T(4,128)S(1)}) fusion(bf16[64,8,2048]{2,1,0:T(8,128)(2,1)} %all-to-all-done), kind=kLoop, calls=%fused_computation.67 | loop fusion | flops 524288 | bytes 5242880 | tf_op jit(solution)/shard_map/slice | solution.py:59
  94.2 1.1 reshape.87
  95.4 4.9 %fusion.26 = f32[256,1536]{1,0:T(8,128)S(1)} fusion(bf16[256,2048]{1,0:T(8,128)(2,1)} %reshape.87, bf16[2048,1536]{1,0:T(8,128)(2,1)} %all-gather.4.cloned.1.call-done), kind=kOutput, calls=%fused_computation.69 | convolution fusion | flops 1610612736 | bytes 8912896 | tf_op jit(solution)/shard_map/dot_general | solution.py:62
  100.3 1.2 copy-done.1
  102.5 8.7 %all-to-all-start.2 = ((f32[64,1,4]{2,1,0:T(1,128)}), f32[64,1,4]{2,1,0:T(1,128)S(1)}, u32[]{:S(2)}, u32[]{:S(2)}) async-start(f32[64,1,4]{2,1,0:T(1,128)} %bitcast.9), calls=%async_computation.2 | async-start | bytes 65536 | tf_op jit(solution)/shard_map/all_to_all | solution.py:11
  111.4 9.0 %all-to-all-done.2 = f32[64,1,4]{2,1,0:T(1,128)S(1)} async-done(((f32[64,1,4]{2,1,0:T(1,128)}), f32[64,1,4]{2,1,0:T(1,128)S(1)}, u32[]{:S(2)}, u32[]{:S(2)}) %all-to-all-start.2) | async-done | bytes 1056 | tf_op jit(solution)/shard_map/all_to_all | solution.py:11
  123.2 4.7 %all-to-all-start.3 = ((f32[64,1,8]{2,1,0:T(1,128)}), f32[64,1,8]{2,1,0:T(1,128)S(1)}, u32[]{:S(2)}, u32[]{:S(2)}) async-start(f32[64,1,8]{2,1,0:T(1,128)} %bitcast.16), calls=%async_computation.3 | async-start | bytes 65536 | tf_op jit(solution)/shard_map/all_to_all | solution.py:11
  128.2 1.7 reshape.92
  129.9 7.4 %all-to-all-done.3 = f32[64,1,8]{2,1,0:T(1,128)S(1)} async-done(((f32[64,1,8]{2,1,0:T(1,128)}), f32[64,1,8]{2,1,0:T(1,128)S(1)}, u32[]{:S(2)}, u32[]{:S(2)}) %all-to-all-start.3) | async-done | bytes 2080 | tf_op jit(solution)/shard_map/all_to_all | solution.py:11
  137.6 4.3 %convolution_convert_fusion = bf16[768,2048]{1,0:T(8,128)(2,1)} fusion(bf16[256,768]{1,0:T(8,128)(2,1)S(1)} %get-tuple-element.29, f32[256,2048]{1,0:T(8,128)} %reshape.92, f32[2048]{0:T(1024)S(1)} %copy-done.7, f32[256]{0:T(256)S(1)} %mul.147, f32[256]{0:T(256)S(1)} %mul.145), kind=kOutput, calls=%fused_computation | convolution fusion | flops 810024960 | bytes 5646336 | tf_op jit(solution)/shard_map/dot_general | solution.py:91
  142.0 1.5 copy-done
  143.5 3.7 %multiply_convert_fusion.2 = (bf16[256,768]{1,0:T(8,128)(2,1)S(1)}, bf16[256,768]{1,0:T(8,128)(2,1)S(1)}, f32[256]{0:T(256)S(1)}) fusion(f32[256,1536]{1,0:T(8,128)} %copy-done.1, bf16[256,768]{1,0:T(8,128)(2,1)S(1)} %get-tuple-element.29, bf16[1,768,2048]{2,1,0:T(8,128)(2,1)} %all-gather.6.cloned.1.call-done, f32[256,2048]{1,0:T(8,128)S(1)} %copy-done, ...), kind=kOutput, calls=%fused_computation.28 | convolution fusion | flops 811597568 | bytes 8006656 | tf_op jit(solution)/shard_map/dot_general | solution.py:96
  147.3 4.6 %convolution_convert_fusion.2 = bf16[256,2048]{1,0:T(8,128)(2,1)S(1)} fusion(bf16[2048,1536]{1,0:T(8,128)(2,1)} %all-gather.4.cloned.1.call-done, bf16[256,768]{1,0:T(8,128)(2,1)S(1)} %get-tuple-element.33, bf16[256,768]{1,0:T(8,128)(2,1)S(1)} %get-tuple-element.32), kind=kOutput, calls=%fused_computation.5 | convolution fusion | flops 1612709888 | bytes 8126464 | tf_op jit(solution)/shard_map/dot_general | solution.py:102
  152.0 1.1 reshape.90
  153.2 9.2 %all-to-all-start.4 = ((bf16[64,4,2176]{2,1,0:T(4,128)(2,1)}), bf16[64,4,2176]{2,1,0:T(4,128)(2,1)S(1)}, u32[]{:S(2)}, u32[]{:S(2)}) async-start(bf16[64,4,2176]{2,1,0:T(4,128)(2,1)} %reshape.90), calls=%async_computation.4 | async-start | bytes 2228224 | tf_op jit(solution)/shard_map/all_to_all | solution.py:11
  162.5 29.8 %all-to-all-done.4 = bf16[64,4,2176]{2,1,0:T(4,128)(2,1)S(1)} async-done(((bf16[64,4,2176]{2,1,0:T(4,128)(2,1)}), bf16[64,4,2176]{2,1,0:T(4,128)(2,1)S(1)}, u32[]{:S(2)}, u32[]{:S(2)}) %all-to-all-start.4) | async-done | bytes 1114144 | tf_op jit(solution)/shard_map/all_to_all | solution.py:11
  193.7 1.0 fusion.3
  194.7 1.9 bitcast_convert_fusion
  (68 shorter events, 9.5 us)
Async XLA Ops:
  7.2 2.3 %copy-start.2 = (bf16[1,96,2048]{2,1,0:T(8,128)(2,1)S(1)}, bf16[1,96,2048]{2,1,0:T(8,128)(2,1)}, u32[]{:S(2)}) copy-start(bf16[1,96,2048]{2,1,0:T(8,128)(2,1)} %param.13) | copy-start | bytes 1179652
  7.2 2.3 %copy-start.7 = (f32[2048]{0:T(1024)S(1)}, f32[2048]{0:T(1024)}, u32[]{:S(2)}) copy-start(f32[2048]{0:T(1024)} %param.14) | copy-start | bytes 24580
  7.2 10.7 %copy-start.8 = (s32[128,1]{0,1:T(1,128)S(1)}, s32[128,1]{0,1:T(1,128)}, u32[]{:S(2)}) copy-start(s32[128,1]{0,1:T(1,128)} %param.15) | copy-start | bytes 1540
  7.2 11.2 %copy-start.5 = (bf16[128,2048]{1,0:T(8,128)(2,1)S(1)}, bf16[128,2048]{1,0:T(8,128)(2,1)}, u32[]{:S(2)}) copy-start(bf16[128,2048]{1,0:T(8,128)(2,1)} %param.10) | copy-start | bytes 1572868
  7.2 11.1 %copy-start.3 = (bf16[128,2048]{1,0:T(8,128)(2,1)S(1)}, bf16[128,2048]{1,0:T(8,128)(2,1)}, u32[]{:S(2)}) copy-start(bf16[128,2048]{1,0:T(8,128)(2,1)} %param.19) | copy-start | bytes 1572868
  7.2 88.1 %all-gather.4.cloned.1.call-start = ((), (), s32[]{:S(2)}) async-start(), calls=%async_computation.6 | async-start | bytes 7077888 | tf_op jit(solution)/shard_map/all_gather | solution.py:45
  10.2 14.1 %all-to-all-start.1 = ((f32[8,1,96]{2,1,0:T(1,128)}), f32[8,1,96]{2,1,0:T(1,128)S(1)}, u32[]{:S(2)}, u32[]{:S(2)}) async-start(f32[8,1,96]{2,1,0:T(1,128)} %broadcast_in_dim.98), calls=%async_computation.1 | async-start | bytes 8192 | tf_op jit(solution)/shard_map/all_to_all | solution.py:50
  24.3 66.8 %all-to-all-start = ((bf16[64,8,2048]{2,1,0:T(8,128)(2,1)}), bf16[64,8,2048]{2,1,0:T(8,128)(2,1)}, u32[]{:S(2)}, u32[]{:S(2)}) async-start(bf16[64,8,2048]{2,1,0:T(8,128)(2,1)} %fusion.2), calls=%async_computation | async-start | bytes 4194304 | tf_op jit(solution)/shard_map/all_to_all | solution.py:11
  40.0 102.0 %all-gather.6.cloned.1.call-start = ((), (), s32[]{:S(2)}) async-start(), calls=%async_computation.8 | async-start | bytes 3538944 | tf_op jit(solution)/shard_map/all_gather | solution.py:48
  100.3 1.2 copy-start.1
  101.5 9.8 %copy-start.6 = (bf16[128,2048]{1,0:T(8,128)(2,1)S(1)}, bf16[128,2048]{1,0:T(8,128)(2,1)}, u32[]{:S(2)}) copy-start(bf16[128,2048]{1,0:T(8,128)(2,1)} %param.10) | copy-start | bytes 1572868
  101.5 20.0 %copy-start.9 = (f32[128,1]{0,1:T(1,128)S(1)}, f32[128,1]{0,1:T(1,128)}, u32[]{:S(2)}) copy-start(f32[128,1]{0,1:T(1,128)} %param.16) | copy-start | bytes 1540
  101.5 20.0 %copy-start.11 = (s32[1,128]{1,0:T(1,128)S(1)}, s32[1,128]{1,0:T(1,128)}, u32[]{:S(2)}) copy-start(s32[1,128]{1,0:T(1,128)} %param.17) | copy-start | bytes 1540
  101.5 20.1 %copy-start.10 = (f32[1,16]{1,0:T(1,128)S(1)}, f32[1,16]{1,0:T(1,128)}, u32[]{:S(2)}) copy-start(f32[1,16]{1,0:T(1,128)} %param.18) | copy-start | bytes 196
  102.5 17.9 %all-to-all-start.2 = ((f32[64,1,4]{2,1,0:T(1,128)}), f32[64,1,4]{2,1,0:T(1,128)S(1)}, u32[]{:S(2)}, u32[]{:S(2)}) async-start(f32[64,1,4]{2,1,0:T(1,128)} %bitcast.9), calls=%async_computation.2 | async-start | bytes 65536 | tf_op jit(solution)/shard_map/all_to_all | solution.py:11
  123.2 14.0 %all-to-all-start.3 = ((f32[64,1,8]{2,1,0:T(1,128)}), f32[64,1,8]{2,1,0:T(1,128)S(1)}, u32[]{:S(2)}, u32[]{:S(2)}) async-start(f32[64,1,8]{2,1,0:T(1,128)} %bitcast.16), calls=%async_computation.3 | async-start | bytes 65536 | tf_op jit(solution)/shard_map/all_to_all | solution.py:11
  127.9 66.7 %reduce-scatter.2.cloned.1.call-start = ((), (), s32[]{:S(2)}) async-start(), calls=%async_computation.7 | async-start | bytes 3538944 | tf_op jit(solution)/shard_map/reduce_scatter | solution.py:94
  141.9 1.6 copy-start
  153.2 39.2 %all-to-all-start.4 = ((bf16[64,4,2176]{2,1,0:T(4,128)(2,1)}), bf16[64,4,2176]{2,1,0:T(4,128)(2,1)S(1)}, u32[]{:S(2)}, u32[]{:S(2)}) async-start(bf16[64,4,2176]{2,1,0:T(4,128)(2,1)} %reshape.90), calls=%async_computation.4 | async-start | bytes 2228224 | tf_op jit(solution)/shard_map/all_to_all | solution.py:11
  162.5 31.2 %copy-start.4 = (bf16[128,2048]{1,0:T(8,128)(2,1)S(1)}, bf16[128,2048]{1,0:T(8,128)(2,1)}, u32[]{:S(2)}) copy-start(bf16[128,2048]{1,0:T(8,128)(2,1)} %param.19) | copy-start | bytes 1572868
Sparse Core Ops, SparseCore 0:
  10.7 82.2 all-gather.3
  95.1 45.8 all-gather.5
  143.8 45.9 reduce-scatter.1

commit v2 on v1

v2 whole, which is shorter than its diff:
```python
import functools

import jax
import jax.numpy as jnp
from jax import lax
from jax.experimental import pallas as pl
from jax.experimental.pallas import tpu as pltpu
from jax.sharding import PartitionSpec as P

BF16 = jnp.bfloat16
F32 = jnp.float32
I32 = jnp.int32
LANES = 128
VMEM = pl.BlockSpec(memory_space=pltpu.VMEM)
SMEM = pl.BlockSpec(memory_space=pltpu.SMEM)
JOIN_FLOPS = 33 * 10**9
EXTRA = 16
NT = (((1,), (1,)), ((), ()))
TN = (((0,), (0,)), ((), ()))


def exchange(rows):
    return lax.all_to_all(rows, "expert", split_axis=0, concat_axis=0, tiled=True)


def shift(block, step):
    count = lax.axis_size("replica")
    return lax.ppermute(block, "replica", [(i, (i + step) % count) for i in range(count)])


def call(body, out_shape, in_specs, flops, moved):
    return pl.pallas_call(
        body,
        out_shape=out_shape,
        in_specs=in_specs,
        out_specs=jax.tree.map(lambda _: VMEM, out_shape),
        cost_estimate=pl.CostEstimate(flops=flops, bytes_accessed=moved, transcendentals=0),
        compiler_params=pltpu.CompilerParams(vmem_limit_bytes=60 * 1024 * 1024),
    )


def iota(shape, axis):
    return lax.broadcasted_iota(I32, shape, axis)


def pack_body(experts, capacity, routes, gates, nodes, tokens, above, out, slot_out):
    rows, width = tokens.shape
    named = routes[...]
    member = (iota((experts, rows), 0) == named).astype(F32)
    before = (iota((rows, rows), 0) < iota((rows, rows), 1)).astype(BF16)
    prior = jnp.dot(member.astype(BF16), before, preferred_element_type=F32)
    rank = jnp.sum(prior * member, axis=0, keepdims=True).astype(I32)
    slot_out[...] = named * capacity + rank
    place = named * (2 * capacity) + rank
    row_of = iota((2 * experts * capacity, rows), 0)
    pick = (row_of == place).astype(BF16)
    pick_above = (row_of == place + capacity).astype(BF16)
    chosen = jnp.dot(pick, tokens[...], preferred_element_type=F32)
    chosen = chosen + jnp.dot(pick_above, above[...], preferred_element_type=F32)
    out[:, :width] = chosen.astype(BF16)
    gate = gates[...]
    high = gate.astype(BF16)
    rest = gate - high.astype(F32)
    middle = rest.astype(BF16)
    low = (rest - middle.astype(F32)).astype(BF16)
    node = nodes[...]
    same = (iota((rows, 16), 1) == node).astype(F32)
    count = jnp.sum(same * jnp.sum(same, axis=0, keepdims=True), axis=1, keepdims=True)
    lane = iota((rows, LANES), 1)
    notes = jnp.where(lane == 0, high.astype(F32), 0.0)
    notes = jnp.where(lane == 1, middle.astype(F32), notes)
    notes = jnp.where(lane == 2, low.astype(F32), notes)
    notes = jnp.where(lane == 3, node.astype(F32), notes)
    notes = jnp.where(lane == 4, count, notes).astype(BF16)
    out[:, width:] = jnp.dot(pick, notes, preferred_element_type=F32).astype(BF16)


def bundle_body(me, gate, down, value_weight, out):
    depth, width = gate.shape
    each = down.shape[0]
    out[:depth, :] = gate[...]
    wanted = value_weight[...]

    def split(value):
        high = value.astype(BF16).astype(F32)
        middle = (value - high).astype(BF16).astype(F32)
        low = (value - high - middle).astype(BF16).astype(F32)
        row = iota((EXTRA, value.shape[1]), 0)
        rows = jnp.where(row == 0, high, jnp.where(row == 1, middle, jnp.where(row == 2, low, 0.0)))
        return rows.astype(BF16)

    three = lax.dot_general(split(wanted), down[...], NT, preferred_element_type=F32)
    head = split(jnp.sum(three, axis=0, keepdims=True))
    place = iota((each, width), 1) == iota((each, width), 0) + me[0] * each
    out[depth:, :] = jnp.dot(head, place.astype(BF16), preferred_element_type=F32).astype(BF16)


def ring_parts(refs, me, count):
    own, far_high, far_low = refs[0], refs[-2], refs[-1]
    rows = own.shape[0]
    parts = [(own, me * rows)]
    for step in range(1, count // 2):
        parts.append((refs[2 * step - 1], lax.rem(me - step + count, count) * rows))
        parts.append((refs[2 * step], lax.rem(me + step, count) * rows))
    far = lax.rem(me + count // 2, count) * rows
    parts.append((far_high, far))
    parts.append((far_low, far + rows // 2))
    return parts


def join_body(count, me, *rest):
    blocks, out = rest[:-1], rest[-1]
    for ref, start in ring_parts(blocks, me[0], count):
        rows = ref.shape[0]
        out[pl.ds(pl.multiple_of(start, 16), rows), :] = ref[...]


def arrive_body(capacity, both, rows, above_out):
    slots, width = above_out.shape
    row = iota((slots, 2 * slots), 0)
    source = row + (row // capacity) * capacity
    column = iota((slots, 2 * slots), 1)
    rows[...] = jnp.dot(
        (column == source).astype(BF16), both[...], preferred_element_type=F32
    ).astype(BF16)
    above = jnp.dot(
        (column == source + capacity).astype(BF16), both[:, :width], preferred_element_type=F32
    )
    above_out[...] = above.astype(BF16)


def forward_body(
    count, capacity, rows, bundles, up, gate_factor, up_factor, hidden_out, note_out, part_out
):
    slots = rows.shape[0]
    width = rows.shape[1] - LANES
    depth = width // count
    gate_act = None
    for owner in range(count):
        part = jnp.dot(
            rows[:, owner * depth : (owner + 1) * depth],
            bundles[owner, :depth, :],
            preferred_element_type=F32,
        )
        gate_act = part if gate_act is None else gate_act + part
    up_act = jnp.dot(rows[:, :width], up[...], preferred_element_type=F32)
    sig = jax.nn.sigmoid(gate_act)
    silu = gate_act * sig
    hidden = (silu * up_act).astype(BF16)
    hidden_out[...] = hidden
    gate_factor[...] = up_act * (sig * (1.0 + gate_act * (1.0 - sig)))
    up_factor[...] = silu
    head = jnp.sum(
        jnp.sum(bundles[:, depth:, :].astype(F32), axis=0), axis=0, keepdims=True
    )
    proj = jnp.sum(hidden.astype(F32) * head, axis=1, keepdims=True)
    notes = rows[:, width:].astype(F32)
    gate = notes[:, 0:1] + notes[:, 1:2] + notes[:, 2:3]
    node = notes[:, 3:4]
    lane = iota((slots, LANES), 1)
    note_out[...] = jnp.where(lane == 0, gate, jnp.where(lane == 1, node, 0.0))
    share = gate * proj / jnp.maximum(notes[:, 4:5], 1.0)
    groups = slots // capacity
    by_node = jnp.where(iota((slots, 16), 1).astype(F32) == node, share, 0.0)
    gather = (iota((groups, slots), 1) // capacity == iota((groups, slots), 0)).astype(F32)
    part_out[...] = jnp.dot(
        gather, by_node, preferred_element_type=F32, precision=lax.Precision.HIGHEST
    )


def partial_body(capacity, sums, notes, above, value_weight, hidden, grad_out, partial_out, error_out):
    slots, width = above.shape
    errors = jnp.sum(sums[...], axis=0, keepdims=True)
    error_out[...] = errors
    lanes = errors.shape[1]
    gate, node = notes[:, 0:1], notes[:, 1:2].astype(I32)
    wanted = (iota((slots, 1), 0) // capacity) * 16 + node
    error = jnp.sum(
        jnp.where(iota((slots, lanes), 1) == wanted, errors, 0.0), axis=1, keepdims=True
    )
    grad = (above[...].astype(F32) + error * value_weight[...]).astype(BF16)
    out_grad = (gate * grad.astype(F32)).astype(BF16)
    grad_out[...] = out_grad
    partial_out[...] = lax.dot_general(
        hidden[...], out_grad, TN, preferred_element_type=F32
    ).astype(BF16)


def backward_body(
    count, grad, down, gate_factor, up_factor, hidden, bundles, up, out, gate_back, up_back
):
    slots, width = grad.shape
    depth = width // count
    hidden_grad = lax.dot_general(grad[...], down[...], NT, preferred_element_type=F32)
    gate_back[...] = (hidden_grad * gate_factor[...]).astype(BF16)
    up_back[...] = (hidden_grad * up_factor[...]).astype(BF16)
    scaled = jnp.sum(hidden[...].astype(F32) * hidden_grad, axis=1, keepdims=True)
    high = scaled.astype(BF16).astype(F32)
    lane = iota((slots, LANES), 1)
    out[:, width:] = jnp.where(
        lane == 0, high, jnp.where(lane == 1, scaled - high, 0.0)
    ).astype(BF16)
    for owner in range(count):
        columns = slice(owner * depth, (owner + 1) * depth)
        part = lax.dot_general(up_back[...], up[columns, :], NT, preferred_element_type=F32)
        part = part + lax.dot_general(
            gate_back[...], bundles[owner, :depth, :], NT, preferred_element_type=F32
        )
        out[:, columns] = part.astype(BF16)


def local(
    tokens,
    gate_weight,
    up_weight,
    down_weight,
    value_weight,
    routes,
    gates,
    node_ids,
    lambda_targets,
    above_grad,
):
    experts = lax.axis_size("expert")
    replicas = lax.axis_size("replica")
    tok_rows, width = tokens.shape
    hidden_width = gate_weight.shape[2]
    capacity = 2 * tok_rows // experts
    slots = experts * capacity
    nodes = lambda_targets.shape[1]
    shape = jax.ShapeDtypeStruct
    value_row = value_weight[None, :]
    me = lax.axis_index("expert")
    my_replica = lax.axis_index("replica").astype(I32).reshape(1)

    bundle = call(
        bundle_body,
        shape((gate_weight.shape[1] + EXTRA, hidden_width), BF16),
        [SMEM, VMEM, VMEM, VMEM],
        0,
        4 * hidden_width * width // replicas,
    )(my_replica, gate_weight[0], down_weight[0], value_row)
    bundles = lax.all_gather(bundle, "replica", axis=0)

    block = up_weight[0]
    blocks = [block]
    right = left = block
    for step in range(1, replicas // 2):
        right, left = shift(right, 1), shift(left, -1)
        blocks += [right, left]
    half = block.shape[0] // 2
    blocks += [shift(right[:half], 1), shift(left[half:], -1)]

    up_full = call(
        functools.partial(join_body, replicas),
        shape((width, hidden_width), BF16),
        [SMEM] + [VMEM] * len(blocks),
        JOIN_FLOPS,
        4 * hidden_width * width,
    )(my_replica, *blocks)

    both, slot_row = call(
        functools.partial(pack_body, experts, capacity),
        [shape((2 * slots, width + LANES), BF16), shape((1, tok_rows), I32)],
        [VMEM] * 5,
        4 * slots * tok_rows * width,
        8 * slots * width,
    )(routes.reshape(1, tok_rows), gates, node_ids.reshape(tok_rows, 1), tokens, above_grad)
    both = exchange(both.reshape(experts, 2 * capacity, width + LANES))
    both = both.reshape(2 * slots, width + LANES)

    rows, above_in = call(
        functools.partial(arrive_body, capacity),
        [shape((slots, width + LANES), BF16), shape((slots, width), BF16)],
        [VMEM],
        4 * slots * slots * width,
        8 * slots * width,
    )(both)
    gate_factor, up_factor, hidden, notes, node_part = call(
        functools.partial(forward_body, replicas, capacity),
        [
            shape((slots, hidden_width), F32),
            shape((slots, hidden_width), F32),
            shape((slots, hidden_width), BF16),
            shape((slots, LANES), F32),
            shape((experts, nodes), F32),
        ],
        [VMEM] * 3,
        4 * slots * hidden_width * width,
        4 * hidden_width * width,
    )(rows, bundles, up_full)
    down = lax.all_gather(down_weight[0], "replica", axis=0, tiled=True)

    in_node = node_ids[0][:, None] == jnp.arange(nodes, dtype=I32)[None, :]
    in_node = in_node.astype(F32)
    token_value = jnp.sum(tokens.astype(F32) * value_row, axis=1)
    own = jnp.sum(in_node * token_value[:, None], axis=0) / jnp.sum(in_node, axis=0)
    own = own - lambda_targets[0]
    is_me = jnp.arange(experts, dtype=I32)[:, None] == me
    node_part = node_part + jnp.where(is_me, own[None, :], 0.0)
    sums = exchange(
        jnp.broadcast_to(node_part.reshape(1, experts * nodes), (experts, experts * nodes))
    )

    out_grad, partial, errors = call(
        functools.partial(partial_body, capacity),
        [
            shape((slots, width), BF16),
            shape((hidden_width, width), BF16),
            shape((1, experts * nodes), F32),
        ],
        [VMEM] * 5,
        2 * slots * hidden_width * width,
        4 * hidden_width * width,
    )(sums, notes, above_in, value_row, hidden)
    down_grad = lax.psum_scatter(partial, "replica", scatter_dimension=0, tiled=True)

    returned, _, _ = call(
        functools.partial(backward_body, replicas),
        [
            shape((slots, width + LANES), BF16),
            shape((slots, hidden_width), BF16),
            shape((slots, hidden_width), BF16),
        ],
        [VMEM] * 7,
        6 * slots * hidden_width * width,
        6 * hidden_width * width,
    )(out_grad, down, gate_factor, up_factor, hidden, bundles, up_full)
    returned = exchange(returned.reshape(experts, capacity, width + LANES))
    returned = returned.reshape(slots, width + LANES)

    node_error = jnp.sum(jnp.where(is_me, errors.reshape(experts, nodes), 0.0), axis=0)
    node_mean = node_error + lambda_targets[0]
    token_error = jnp.sum(in_node * node_error[None, :], axis=1)
    at_slot = slot_row.reshape(tok_rows, 1) == jnp.arange(slots, dtype=I32)[None, :]
    route_rows = jnp.dot(at_slot.astype(BF16), returned, preferred_element_type=F32)
    value_grad = (above_grad.astype(F32) + token_error[:, None] * value_row).astype(BF16)
    token_grad = (value_grad.astype(F32) + route_rows[:, :width]).astype(BF16)
    gate_grad = (route_rows[:, width : width + 1] + route_rows[:, width + 1 : width + 2]) / gates
    return token_grad, gate_grad, down_grad.astype(F32)[None], node_mean[None, :]


def solution(mesh):
    rows = P(("expert", "replica"), None)
    weight = P("expert", "replica", None)
    return jax.shard_map(
        local,
        mesh=mesh,
        in_specs=(rows, weight, weight, weight, P(), rows, rows, rows, rows, rows),
        out_specs=(rows, rows, weight, rows),
        check_vma=False,
    )
```

time: 204 us -> 197 us (0.966)
  waiting for transfers between devices: 99.9 us -> 60.6 us
  Pallas kernels: 0 us -> 33.9 us
  blocking collectives: 0 us -> 24.3 us
  matrix products: 20 us -> 0.37 us
  other arithmetic: 12.8 us -> 6.23 us
    all_to_all x4 -> x2, waiting for transfers between devices: 95.3 us -> 28 us  [exchange(): lax.all_to_all(rows, 'expert', split_axis=0, concat_axis=0, tiled=True)]
    pallas_call x0 -> x7, Pallas kernels: none -> 33.9 us  [the longest x1 9.07 us: local(): call(functools.partial(backward_body, replicas), [shape((slots, width + L...]
    ppermute x0 -> x8, waiting for transfers between devices: none -> 32.5 us  [shift(): lax.ppermute(block, 'replica', [(i, (i + step) % count) for i in range(co...]
    ppermute x0 -> x8, starting transfers between devices: none -> 27.3 us  [shift(): lax.ppermute(block, 'replica', [(i, (i + step) % count) for i in range(co...]
    all_to_all x0 -> x1, blocking collectives: none -> 24.3 us  [exchange(): lax.all_to_all(rows, 'expert', split_axis=0, concat_axis=0, tiled=True)]
    dot_general x5 -> x0, matrix products: 19.7 us -> none  [the longest x1 4.9 us: local(): acts = jnp.dot(rows_in, gate_up, preferred_element_type=F32)]
    all_to_all x4 -> x2, starting transfers between devices: 38.2 us -> 20.5 us  [exchange(): lax.all_to_all(rows, 'expert', split_axis=0, concat_axis=0, tiled=True)]
    all_to_all x1 -> x0, starting transfers between devices: 7.65 us -> none  [local(): lax.all_to_all(jnp.broadcast_to(head_part[None, :], (replicas, hidden_wid...]
  transfers between devices with their start and end apart: 8 -> 13, of which waited for: 5 -> 5; matrix products, arithmetic and copies ran while one was open for 17% -> 6% of each run, Pallas kernels for 0% -> 16%
where the time goes in v2:
time: 197 us; the launch traced here: 196 us
  waiting for transfers between devices  60.6 us (31%)
  starting transfers between devices  47.9 us (24%)
  Pallas kernels  33.9 us (17%)
  blocking collectives  24.3 us (12%)
  between operations  14.1 us (7%)
  local copies, waits for them, and re-layouts  8.71 us (4%)
  other arithmetic  6.23 us (3%)
    ppermute x8, waiting for transfers between devices, shift(): lax.ppermute(block, 'replica', [(i, (i + step) % count) for i in range(co...  32.5 us
    all_to_all x2, waiting for transfers between devices, exchange(): lax.all_to_all(rows, 'expert', split_axis=0, concat_axis=0, tiled=True)  28 us
    ppermute x8, starting transfers between devices, shift(): lax.ppermute(block, 'replica', [(i, (i + step) % count) for i in range(co...  27.3 us
    all_to_all x1, blocking collectives, exchange(): lax.all_to_all(rows, 'expert', split_axis=0, concat_axis=0, tiled=True)  24.3 us
    all_to_all x2, starting transfers between devices, exchange(): lax.all_to_all(rows, 'expert', split_axis=0, concat_axis=0, tiled=True)  20.5 us
    pallas_call x1, Pallas kernels, local(): call(functools.partial(backward_body, replicas), [shape((slots, width + L...  9.07 us
    pallas_call x1, Pallas kernels, local(): call(functools.partial(forward_body, replicas, capacity), [shape((slots,...  6.19 us
    unnamed x37, local copies, waits for them, and re-layouts  4.59 us
  transfers between devices with their start and end apart: 13, of which 5 were waited for; matrix products, arithmetic and copies ran while one was open for 6% of the time, Pallas kernels for 16%

profile of v2, /device:TPU:1, one launch (start us, length us, event | category | flops | bytes accessed | tf_op | source)
XLA Modules:
  0.0 196.1 jit_solution(6633473944345339128)
XLA Ops:
  7.2 2.3 %shard_map.131 = bf16[272,768]{1,0:T(8,128)(2,1)} custom-call(s32[1]{0:T(128)} %bitcast.5.me, bf16[256,768]{1,0:T(8,128)(2,1)} %bitcast.34, bf16[96,2048]{1,0:T(8,128)(2,1)} %bitcast.33, f32[1,2048]{1,0:T(1,128)} %bitcast.36), custom_call_target="tpu_custom_call" | custom-call | bytes 786432 | tf_op jit(solution)/shard_map/pallas_call | solution.py:236
  9.7 4.0 %collective-permute-start = (bf16[256,768]{1,0:T(8,128)(2,1)S(1)}, bf16[256,768]{1,0:T(8,128)(2,1)S(1)}, u32[]{:S(2)}, u32[]{:S(2)}) collective-permute-start(bf16[256,768]{1,0:T(8,128)(2,1)S(1)} %bitcast.44), channel_id=1, source_target_pairs={{0,1},{1,2},{2,3},{3,4},{4,5},{5,6},{6,7},{7,0},{8,9},{9,10},{10,1... | collective-permute-start | bytes 1179656 | tf_op jit(solution)/shard_map/ppermute | solution.py:28
  13.7 3.8 %collective-permute-start.1 = (bf16[256,768]{1,0:T(8,128)(2,1)S(1)}, bf16[256,768]{1,0:T(8,128)(2,1)}, u32[]{:S(2)}, u32[]{:S(2)}) collective-permute-start(bf16[256,768]{1,0:T(8,128)(2,1)S(1)} %bitcast.45), channel_id=1, source_target_pairs={{0,7},{1,0},{2,1},{3,2},{4,3},{5,4},{6,5},{7,6},{8,15},{9,8},{10,9... | collective-permute-start | bytes 1179656 | tf_op jit(solution)/shard_map/ppermute | solution.py:28
  19.1 4.1 %shard_map.129 = (bf16[512,2176]{1,0:T(8,128)(2,1)}, s32[1,128]{1,0:T(1,128)}) custom-call(s32[1,128]{1,0:T(1,128)} %bitcast.41, f32[128,1]{1,0:T(8,128)} %copy.26.gates, s32[128,1]{1,0:T(8,128)} %copy.27.nodes, bf16[128,2048]{1,0:T(8,128)(2,1)} %tokens.1, bf16[128,2048]{1,0:T(8,128)(2,1)} %above.1), custom_call_target="tpu_custom_call" | custom-call | flops 268435456 | bytes 4194304 | tf_op jit(solution)/shard_map/pallas_call | solution.py:262
  23.1 14.4 %all-to-all-start = ((bf16[64,8,2176]{2,1,0:T(8,128)(2,1)}), bf16[64,8,2176]{2,1,0:T(8,128)(2,1)S(1)}, u32[]{:S(2)}, u32[]{:S(2)}) async-start(bf16[64,8,2176]{2,1,0:T(8,128)(2,1)} %bitcast.32), calls=%async_computation | async-start | bytes 4456448 | tf_op jit(solution)/shard_map/all_to_all | solution.py:23
  37.6 1.9 collective-permute-start.2
  39.5 4.6 %collective-permute-start.3 = (bf16[256,768]{1,0:T(8,128)(2,1)}, bf16[256,768]{1,0:T(8,128)(2,1)}, u32[]{:S(2)}, u32[]{:S(2)}) collective-permute-start(bf16[256,768]{1,0:T(8,128)(2,1)} %collective-permute-done.1.rest_2_), channel_id=1, source_target_pairs={{0,7},{1,0},{2,1},{3,2},{4,3},{5,4},{6,5},{7,6},{8,15},{9,8},{10,9... | collective-permute-start | bytes 1179656 | tf_op jit(solution)/shard_map/ppermute | solution.py:28
  44.1 15.9 %collective-permute-done.2.rest_3_ = bf16[256,768]{1,0:T(8,128)(2,1)} collective-permute-done((bf16[256,768]{1,0:T(8,128)(2,1)S(1)}, bf16[256,768]{1,0:T(8,128)(2,1)}, u32[]{:S(2)}, u32[]{:S(2)}) %collective-permute-start.2) | collective-permute-done | bytes 393248 | tf_op jit(solution)/shard_map/ppermute | solution.py:28
  60.0 1.9 collective-permute-start.4
  62.0 4.6 %collective-permute-start.5 = (bf16[256,768]{1,0:T(8,128)(2,1)}, bf16[256,768]{1,0:T(8,128)(2,1)S(1)}, u32[]{:S(2)}, u32[]{:S(2)}) collective-permute-start(bf16[256,768]{1,0:T(8,128)(2,1)} %collective-permute-done.3.rest_4_), channel_id=1, source_target_pairs={{0,7},{1,0},{2,1},{3,2},{4,3},{5,4},{6,5},{7,6},{8,15},{9,8},{10,9... | collective-permute-start | bytes 1179656 | tf_op jit(solution)/shard_map/ppermute | solution.py:28
  66.9 14.4 %collective-permute-done.4.rest_5_ = bf16[256,768]{1,0:T(8,128)(2,1)S(1)} collective-permute-done((bf16[256,768]{1,0:T(8,128)(2,1)}, bf16[256,768]{1,0:T(8,128)(2,1)S(1)}, u32[]{:S(2)}, u32[]{:S(2)}) %collective-permute-start.4) | collective-permute-done | bytes 393248 | tf_op jit(solution)/shard_map/ppermute | solution.py:28
  81.3 1.9 collective-permute-start.6
  83.3 4.6 %collective-permute-start.7 = (bf16[128,768]{1,0:T(8,128)(2,1)S(1)}, bf16[128,768]{1,0:T(8,128)(2,1)S(1)}, u32[]{:S(2)}, u32[]{:S(2)}) collective-permute-start(bf16[128,768]{1,0:T(8,128)(2,1)S(1)} %slice.21), channel_id=1, source_target_pairs={{0,7},{1,0},{2,1},{3,2},{4,3},{5,4},{6,5},{7,6},{8,15},{9,8},{10,9... | collective-permute-start | bytes 589832 | tf_op jit(solution)/shard_map/ppermute | solution.py:28
  91.5 3.7 %shard_map.132.up = bf16[2048,768]{1,0:T(8,128)(2,1)} custom-call(s32[1]{0:T(128)} %bitcast.5.me, bf16[256,768]{1,0:T(8,128)(2,1)} %bitcast.43, bf16[256,768]{1,0:T(8,128)(2,1)} %copy-done.14, bf16[256,768]{1,0:T(8,128)(2,1)} %collective-permute-done.1.rest_2_, bf16[256,768]{1,0:T(8,128)(2,1)} %collective-permute-done.2.rest_3_, ...), custom_call_target="tpu_custom_call" | custom-call | flops 32999999488 | bytes 6291456 | tf_op jit(solution)/shard_map/pallas_call | solution.py:254
  95.2 1.3 copy-done
  96.5 4.0 %shard_map.130 = (bf16[256,2176]{1,0:T(8,128)(2,1)}, bf16[256,2048]{1,0:T(8,128)(2,1)}) custom-call(bf16[512,2176]{1,0:T(8,128)(2,1)} %bitcast.30), custom_call_target="tpu_custom_call" | custom-call | flops 536870912 | bytes 4194304 | tf_op jit(solution)/shard_map/pallas_call | solution.py:272
  100.5 6.2 %shard_map.133 = (f32[256,768]{1,0:T(8,128)}, f32[256,768]{1,0:T(8,128)}, bf16[256,768]{1,0:T(8,128)(2,1)}, f32[256,128]{1,0:T(8,128)}, f32[64,16]{1,0:T(8,128)}) custom-call(bf16[256,2176]{1,0:T(8,128)(2,1)} %get-tuple-element.18.rows, bf16[8,272,768]{2,1,0:T(8,128)(2,1)} %bitcast.28, bf16[2048,768]{1,0:T(8,128)(2,1)} %shard_map.132.up), custom_call_target="tpu_custom_call" | custom-call | flops 1610612736 | bytes 6291456 | tf_op jit(solution)/shard_map/pallas_call | solution.py:279
  107.8 24.3 %all_to_all.18 = f32[64,1,1024]{2,1,0:T(1,128)S(1)} all-to-all(f32[64,1,1024]{2,1,0:T(1,128)S(1)} %broadcast_in_dim.60), channel_id=1, replica_groups=mesh['expert'=64,'replica'=8] {'expert'}, dimensions={0} | all-to-all | bytes 524288 | tf_op jit(solution)/shard_map/all_to_all | solution.py:23
  132.9 4.5 %shard_map.134 = (bf16[256,2048]{1,0:T(8,128)(2,1)}, bf16[768,2048]{1,0:T(8,128)(2,1)}, f32[1,1024]{1,0:T(1,128)}) custom-call(f32[64,1024]{1,0:T(8,128)} %bitcast.35, f32[256,128]{1,0:T(8,128)} %get-tuple-element.20.notes, bf16[256,2048]{1,0:T(8,128)(2,1)} %get-tuple-element.21.above, f32[1,2048]{1,0:T(1,128)} %bitcast.37, ...), custom_call_target="tpu_custom_call" | custom-call | flops 805306368 | bytes 6291456 | tf_op jit(solution)/shard_map/pallas_call | solution.py:305
  137.4 9.1 %shard_map.135 = (bf16[256,2176]{1,0:T(8,128)(2,1)}, bf16[256,768]{1,0:T(8,128)(2,1)}, bf16[256,768]{1,0:T(8,128)(2,1)}) custom-call(bf16[256,2048]{1,0:T(8,128)(2,1)} %get-tuple-element.25.grad, bf16[768,2048]{1,0:T(8,128)(2,1)} %bitcast.31, f32[256,768]{1,0:T(8,128)} %get-tuple-element.26.gate_factor, f32[256,768]{1,0:T(8,128)} %get-tuple-element.27.up_factor, ...), custom_call_target="tpu_custom_call" | custom-call | flops 2415919104 | bytes 9437184 | tf_op jit(solution)/shard_map/pallas_call | solution.py:318
  146.5 2.3 %reshape.73 = bf16[64,4,2176]{2,1,0:T(4,128)(2,1)} reshape(bf16[256,2176]{1,0:T(8,128)(2,1)} %get-tuple-element.28) | data formatting | bytes 2228224 | tf_op jit(solution)/shard_map/reshape | solution.py:329
  148.8 6.1 %all-to-all-start.2 = ((bf16[64,4,2176]{2,1,0:T(4,128)(2,1)}), bf16[64,4,2176]{2,1,0:T(4,128)(2,1)S(1)}, u32[]{:S(2)}, u32[]{:S(2)}) async-start(bf16[64,4,2176]{2,1,0:T(4,128)(2,1)} %reshape.73), calls=%async_computation.2 | async-start | bytes 2228224 | tf_op jit(solution)/shard_map/all_to_all | solution.py:23
  156.8 28.0 %all-to-all-done.2 = bf16[64,4,2176]{2,1,0:T(4,128)(2,1)S(1)} async-done(((bf16[64,4,2176]{2,1,0:T(4,128)(2,1)}), bf16[64,4,2176]{2,1,0:T(4,128)(2,1)S(1)}, u32[]{:S(2)}, u32[]{:S(2)}) %all-to-all-start.2) | async-done | bytes 1114144 | tf_op jit(solution)/shard_map/all_to_all | solution.py:23
  187.7 1.9 bitcast_convert_fusion
  (72 shorter events, 12.2 us)
Async XLA Ops:
  7.2 2.5 %copy-start.13 = (bf16[1,256,768]{2,1,0:T(8,128)(2,1)S(1)}, bf16[1,256,768]{2,1,0:T(8,128)(2,1)}, u32[]{:S(2)}) copy-start(bf16[1,256,768]{2,1,0:T(8,128)(2,1)} %param.12) | copy-start | bytes 1179652
  7.2 10.4 %copy-start.10 = (f32[128,1]{0,1:T(1,128)S(1)}, f32[128,1]{0,1:T(1,128)}, u32[]{:S(2)}) copy-start(f32[128,1]{0,1:T(1,128)} %param.16) | copy-start | bytes 1540
  7.2 11.1 %copy-start.9 = (s32[1,128]{1,0:T(1,128)S(1)}, s32[1,128]{1,0:T(1,128)}, u32[]{:S(2)}) copy-start(s32[1,128]{1,0:T(1,128)} %param.17) | copy-start | bytes 1540
  7.2 93.3 %all-gather.5.cloned.1.call-start = ((), (), s32[]{:S(2)}) async-start(), calls=%async_computation.5 | async-start | bytes 3760128 | tf_op jit(solution)/shard_map/all_gather | solution.py:243
  9.6 127.8 %all-gather.7.cloned.1.call-start = ((), (), s32[]{:S(2)}) async-start(), calls=%async_computation.6 | async-start | bytes 3538944 | tf_op jit(solution)/shard_map/all_gather | solution.py:292
  9.7 27.9 %collective-permute-start = (bf16[256,768]{1,0:T(8,128)(2,1)S(1)}, bf16[256,768]{1,0:T(8,128)(2,1)S(1)}, u32[]{:S(2)}, u32[]{:S(2)}) collective-permute-start(bf16[256,768]{1,0:T(8,128)(2,1)S(1)} %bitcast.44), channel_id=1, source_target_pairs={{0,1},{1,2},{2,3},{3,4},{4,5},{5,6},{6,7},{7,0},{8,9},{9,10},{10,1... | collective-permute-start | bytes 1179656 | tf_op jit(solution)/shard_map/ppermute | solution.py:28
  13.7 25.8 %collective-permute-start.1 = (bf16[256,768]{1,0:T(8,128)(2,1)S(1)}, bf16[256,768]{1,0:T(8,128)(2,1)}, u32[]{:S(2)}, u32[]{:S(2)}) collective-permute-start(bf16[256,768]{1,0:T(8,128)(2,1)S(1)} %bitcast.45), channel_id=1, source_target_pairs={{0,7},{1,0},{2,1},{3,2},{4,3},{5,4},{6,5},{7,6},{8,15},{9,8},{10,9... | collective-permute-start | bytes 1179656 | tf_op jit(solution)/shard_map/ppermute | solution.py:28
  23.1 43.5 %copy-start.2 = (bf16[128,2048]{1,0:T(8,128)(2,1)S(1)}, bf16[128,2048]{1,0:T(8,128)(2,1)}, u32[]{:S(2)}) copy-start(bf16[128,2048]{1,0:T(8,128)(2,1)} %tokens.1) | copy-start | bytes 1572868
  23.1 43.5 %copy-start.6 = (f32[2048]{0:T(1024)S(1)}, f32[2048]{0:T(1024)}, u32[]{:S(2)}) copy-start(f32[2048]{0:T(1024)} %param.14) | copy-start | bytes 24580
  23.1 72.1 %all-to-all-start = ((bf16[64,8,2176]{2,1,0:T(8,128)(2,1)}), bf16[64,8,2176]{2,1,0:T(8,128)(2,1)S(1)}, u32[]{:S(2)}, u32[]{:S(2)}) async-start(bf16[64,8,2176]{2,1,0:T(8,128)(2,1)} %bitcast.32), calls=%async_computation | async-start | bytes 4456448 | tf_op jit(solution)/shard_map/all_to_all | solution.py:23
  37.5 150.1 %reduce-scatter.2.cloned.1.call-start = ((), (), s32[]{:S(2)}) async-start(), calls=%async_computation.4 | async-start | bytes 3538944 | tf_op jit(solution)/shard_map/reduce_scatter | solution.py:316
  37.6 24.4 %copy-start.14 = (bf16[256,768]{1,0:T(8,128)(2,1)}, bf16[256,768]{1,0:T(8,128)(2,1)S(1)}, u32[]{:S(2)}) copy-start(bf16[256,768]{1,0:T(8,128)(2,1)S(1)} %collective-permute-done.rest_1_) | copy-start | bytes 1179652
  37.6 22.4 %collective-permute-start.2 = (bf16[256,768]{1,0:T(8,128)(2,1)S(1)}, bf16[256,768]{1,0:T(8,128)(2,1)}, u32[]{:S(2)}, u32[]{:S(2)}) collective-permute-start(bf16[256,768]{1,0:T(8,128)(2,1)S(1)} %collective-permute-done.rest_1_), channel_id=1, source_target_pairs={{0,1},{1,2},{2,3},{3,4},{4,5},{5,6},{6,7},{7,0},{8,9},{9,10},{10,1... | collective-permute-start | bytes 1179656 | tf_op jit(solution)/shard_map/ppermute | solution.py:28
  39.5 22.4 %collective-permute-start.3 = (bf16[256,768]{1,0:T(8,128)(2,1)}, bf16[256,768]{1,0:T(8,128)(2,1)}, u32[]{:S(2)}, u32[]{:S(2)}) collective-permute-start(bf16[256,768]{1,0:T(8,128)(2,1)} %collective-permute-done.1.rest_2_), channel_id=1, source_target_pairs={{0,7},{1,0},{2,1},{3,2},{4,3},{5,4},{6,5},{7,6},{8,15},{9,8},{10,9... | collective-permute-start | bytes 1179656 | tf_op jit(solution)/shard_map/ppermute | solution.py:28
  60.0 21.2 %collective-permute-start.4 = (bf16[256,768]{1,0:T(8,128)(2,1)}, bf16[256,768]{1,0:T(8,128)(2,1)S(1)}, u32[]{:S(2)}, u32[]{:S(2)}) collective-permute-start(bf16[256,768]{1,0:T(8,128)(2,1)} %collective-permute-done.2.rest_3_), channel_id=1, source_target_pairs={{0,1},{1,2},{2,3},{3,4},{4,5},{5,6},{6,7},{7,0},{8,9},{9,10},{10,1... | collective-permute-start | bytes 1179656 | tf_op jit(solution)/shard_map/ppermute | solution.py:28
  62.0 21.2 %collective-permute-start.5 = (bf16[256,768]{1,0:T(8,128)(2,1)}, bf16[256,768]{1,0:T(8,128)(2,1)S(1)}, u32[]{:S(2)}, u32[]{:S(2)}) collective-permute-start(bf16[256,768]{1,0:T(8,128)(2,1)} %collective-permute-done.3.rest_4_), channel_id=1, source_target_pairs={{0,7},{1,0},{2,1},{3,2},{4,3},{5,4},{6,5},{7,6},{8,15},{9,8},{10,9... | collective-permute-start | bytes 1179656 | tf_op jit(solution)/shard_map/ppermute | solution.py:28
  81.3 9.5 %copy-start.4 = (bf16[256,768]{1,0:T(8,128)(2,1)}, bf16[256,768]{1,0:T(8,128)(2,1)S(1)}, u32[]{:S(2)}) copy-start(bf16[256,768]{1,0:T(8,128)(2,1)S(1)} %collective-permute-done.4.rest_5_) | copy-start | bytes 1179652
  81.3 8.5 %collective-permute-start.6 = (bf16[128,768]{1,0:T(8,128)(2,1)S(1)}, bf16[128,768]{1,0:T(8,128)(2,1)S(1)}, u32[]{:S(2)}, u32[]{:S(2)}) collective-permute-start(bf16[128,768]{1,0:T(8,128)(2,1)S(1)} %slice.20), channel_id=1, source_target_pairs={{0,1},{1,2},{2,3},{3,4},{4,5},{5,6},{6,7},{7,0},{8,9},{9,10},{10,1... | collective-permute-start | bytes 589832 | tf_op jit(solution)/shard_map/ppermute | solution.py:28
  83.2 7.5 %copy-start.5 = (bf16[256,768]{1,0:T(8,128)(2,1)}, bf16[256,768]{1,0:T(8,128)(2,1)S(1)}, u32[]{:S(2)}) copy-start(bf16[256,768]{1,0:T(8,128)(2,1)S(1)} %collective-permute-done.5.rest_6_) | copy-start | bytes 1179652
  83.3 7.5 %collective-permute-start.7 = (bf16[128,768]{1,0:T(8,128)(2,1)S(1)}, bf16[128,768]{1,0:T(8,128)(2,1)S(1)}, u32[]{:S(2)}, u32[]{:S(2)}) collective-permute-start(bf16[128,768]{1,0:T(8,128)(2,1)S(1)} %slice.21), channel_id=1, source_target_pairs={{0,7},{1,0},{2,1},{3,2},{4,3},{5,4},{6,5},{7,6},{8,15},{9,8},{10,9... | collective-permute-start | bytes 589832 | tf_op jit(solution)/shard_map/ppermute | solution.py:28
  148.8 6.6 %copy-start.8 = (f32[1,1024]{1,0:T(1,128)S(1)}, f32[1,1024]{1,0:T(1,128)}, u32[]{:S(2)}) copy-start(f32[1,1024]{1,0:T(1,128)} %get-tuple-element.23) | copy-start | bytes 12292
  148.8 7.5 %copy-start.12 = (f32[1,16]{1,0:T(1,128)S(1)}, f32[1,16]{1,0:T(1,128)}, u32[]{:S(2)}) copy-start(f32[1,16]{1,0:T(1,128)} %param.18) | copy-start | bytes 196
  148.8 36.1 %all-to-all-start.2 = ((bf16[64,4,2176]{2,1,0:T(4,128)(2,1)}), bf16[64,4,2176]{2,1,0:T(4,128)(2,1)S(1)}, u32[]{:S(2)}, u32[]{:S(2)}) async-start(bf16[64,4,2176]{2,1,0:T(4,128)(2,1)} %reshape.73), calls=%async_computation.2 | async-start | bytes 2228224 | tf_op jit(solution)/shard_map/all_to_all | solution.py:23
  156.8 28.3 %copy-start.11 = (s32[1,128]{1,0:T(1,128)S(1)}, s32[1,128]{1,0:T(1,128)}, u32[]{:S(2)}) copy-start(s32[1,128]{1,0:T(1,128)} %get-tuple-element.24) | copy-start | bytes 1540
  (6 other events, 6.8 us)
Sparse Core Ops, SparseCore 0:
  10.7 69.6 all-gather.4
  82.4 46.9 all-gather.6
  137.5 41.5 reduce-scatter.1

commit v3 on v2

--- a/solution.py
+++ b/solution.py
@@ -95,28 +95,25 @@
     out[depth:, :] = jnp.dot(head, place.astype(BF16), preferred_element_type=F32).astype(BF16)
 
 
-def ring_parts(refs, me, count):
-    own, far_high, far_low = refs[0], refs[-2], refs[-1]
-    rows = own.shape[0]
-    parts = [(own, me * rows)]
+def ring_owners(me, count):
+    owners = [me]
     for step in range(1, count // 2):
-        parts.append((refs[2 * step - 1], lax.rem(me - step + count, count) * rows))
-        parts.append((refs[2 * step], lax.rem(me + step, count) * rows))
-    far = lax.rem(me + count // 2, count) * rows
-    parts.append((far_high, far))
-    parts.append((far_low, far + rows // 2))
-    return parts
-
-
-def join_body(count, me, *rest):
-    blocks, out = rest[:-1], rest[-1]
-    for ref, start in ring_parts(blocks, me[0], count):
-        rows = ref.shape[0]
-        out[pl.ds(pl.multiple_of(start, 16), rows), :] = ref[...]
-
-
-def arrive_body(capacity, both, rows, above_out):
+        owners.append(lax.rem(me - step + count, count))
+        owners.append(lax.rem(me + step, count))
+    return owners + [lax.rem(me + count // 2, count)]
+
+
+def join_body(high, low, out):
+    rows = high.shape[0]
+    out[:rows, :] = high[...]
+    out[rows:, :] = low[...]
+
+
+def forward_body(count, capacity, me, both, bundles, *rest):
+    blocks, rest = rest[:count], rest[count:]
+    above_out, gate_factor, up_factor, hidden_out, note_out, part_out, rows = rest
     slots, width = above_out.shape
+    depth = width // count
     row = iota((slots, 2 * slots), 0)
     source = row + (row // capacity) * capacity
     column = iota((slots, 2 * slots), 1)
@@ -127,14 +124,11 @@
         (column == source + capacity).astype(BF16), both[:, :width], preferred_element_type=F32
     )
     above_out[...] = above.astype(BF16)
-
-
-def forward_body(
-    count, capacity, rows, bundles, up, gate_factor, up_factor, hidden_out, note_out, part_out
-):
-    slots = rows.shape[0]
-    width = rows.shape[1] - LANES
-    depth = width // count
+    up_act = None
+    for owner, ref in zip(ring_owners(me[0], count), blocks, strict=True):
+        columns = pl.ds(pl.multiple_of(owner * depth, 128), depth)
+        part = jnp.dot(rows[:, columns], ref[...], preferred_element_type=F32)
+        up_act = part if up_act is None else up_act + part
     gate_act = None
     for owner in range(count):
         part = jnp.dot(
@@ -143,13 +137,12 @@
             preferred_element_type=F32,
         )
         gate_act = part if gate_act is None else gate_act + part
-    up_act = jnp.dot(rows[:, :width], up[...], preferred_element_type=F32)
     sig = jax.nn.sigmoid(gate_act)
     silu = gate_act * sig
     hidden = (silu * up_act).astype(BF16)
     hidden_out[...] = hidden
-    gate_factor[...] = up_act * (sig * (1.0 + gate_act * (1.0 - sig)))
-    up_factor[...] = silu
+    gate_factor[...] = (up_act * (sig * (1.0 + gate_act * (1.0 - sig)))).astype(BF16)
+    up_factor[...] = silu.astype(BF16)
     head = jnp.sum(
         jnp.sum(bundles[:, depth:, :].astype(F32), axis=0), axis=0, keepdims=True
     )
@@ -186,27 +179,36 @@
     ).astype(BF16)
 
 
-def backward_body(
-    count, grad, down, gate_factor, up_factor, hidden, bundles, up, out, gate_back, up_back
-):
+def backward_body(count, me, grad, down, gate_factor, up_factor, hidden, bundles, *rest):
+    blocks, (out, gate_back, up_back) = rest[:count], rest[count:]
     slots, width = grad.shape
     depth = width // count
     hidden_grad = lax.dot_general(grad[...], down[...], NT, preferred_element_type=F32)
-    gate_back[...] = (hidden_grad * gate_factor[...]).astype(BF16)
-    up_back[...] = (hidden_grad * up_factor[...]).astype(BF16)
+    gate_back[...] = (hidden_grad * gate_factor[...].astype(F32)).astype(BF16)
+    up_back[...] = (hidden_grad * up_factor[...].astype(F32)).astype(BF16)
     scaled = jnp.sum(hidden[...].astype(F32) * hidden_grad, axis=1, keepdims=True)
     high = scaled.astype(BF16).astype(F32)
     lane = iota((slots, LANES), 1)
     out[:, width:] = jnp.where(
         lane == 0, high, jnp.where(lane == 1, scaled - high, 0.0)
     ).astype(BF16)
-    for owner in range(count):
-        columns = slice(owner * depth, (owner + 1) * depth)
-        part = lax.dot_general(up_back[...], up[columns, :], NT, preferred_element_type=F32)
+    for owner, ref in zip(ring_owners(me[0], count), blocks, strict=True):
+        part = lax.dot_general(up_back[...], ref[...], NT, preferred_element_type=F32)
         part = part + lax.dot_general(
             gate_back[...], bundles[owner, :depth, :], NT, preferred_element_type=F32
         )
-        out[:, columns] = part.astype(BF16)
+        out[:, pl.ds(pl.multiple_of(owner * depth, 128), depth)] = part.astype(BF16)
+
+
+def finish_body(returned, slot, above, value_weight, error, gates, sums, token_out, gate_out, down_out):
+    slots = returned.shape[0]
+    rows, width = above.shape
+    pick = (iota((slots, rows), 0) == slot[...]).astype(BF16)
+    mine = lax.dot_general(pick, returned[...], TN, preferred_element_type=F32)
+    grad = (above[...].astype(F32) + error[...] * value_weight[...]).astype(BF16)
+    token_out[...] = (grad.astype(F32) + mine[:, :width]).astype(BF16)
+    gate_out[...] = (mine[:, width : width + 1] + mine[:, width + 1 : width + 2]) / gates[...]
+    down_out[...] = sums[...].astype(F32)
 
 
 def local(
@@ -251,13 +253,11 @@
     half = block.shape[0] // 2
     blocks += [shift(right[:half], 1), shift(left[half:], -1)]
 
-    up_full = call(
-        functools.partial(join_body, replicas),
-        shape((width, hidden_width), BF16),
-        [SMEM] + [VMEM] * len(blocks),
-        JOIN_FLOPS,
-        4 * hidden_width * width,
-    )(my_replica, *blocks)
+    blocks[-2:] = [
+        call(join_body, shape(block.shape, BF16), [VMEM] * 2, JOIN_FLOPS, 4 * half * hidden_width)(
+            *blocks[-2:]
+        )
+    ]
 
     both, slot_row = call(
         functools.partial(pack_body, experts, capacity),
@@ -269,26 +269,21 @@
     both = exchange(both.reshape(experts, 2 * capacity, width + LANES))
     both = both.reshape(2 * slots, width + LANES)
 
-    rows, above_in = call(
-        functools.partial(arrive_body, capacity),
-        [shape((slots, width + LANES), BF16), shape((slots, width), BF16)],
-        [VMEM],
-        4 * slots * slots * width,
-        8 * slots * width,
-    )(both)
-    gate_factor, up_factor, hidden, notes, node_part = call(
+    above_in, gate_factor, up_factor, hidden, notes, node_part, _ = call(
         functools.partial(forward_body, replicas, capacity),
         [
-            shape((slots, hidden_width), F32),
-            shape((slots, hidden_width), F32),
+            shape((slots, width), BF16),
+            shape((slots, hidden_width), BF16),
+            shape((slots, hidden_width), BF16),
             shape((slots, hidden_width), BF16),
             shape((slots, LANES), F32),
             shape((experts, nodes), F32),
+            shape((slots, width + LANES), BF16),
         ],
-        [VMEM] * 3,
+        [SMEM] + [VMEM] * (2 + replicas),
         4 * slots * hidden_width * width,
         4 * hidden_width * width,
-    )(rows, bundles, up_full)
+    )(my_replica, both, bundles, *blocks)
     down = lax.all_gather(down_weight[0], "replica", axis=0, tiled=True)
 
     in_node = node_ids[0][:, None] == jnp.arange(nodes, dtype=I32)[None, :]
@@ -322,22 +317,28 @@
             shape((slots, hidden_width), BF16),
             shape((slots, hidden_width), BF16),
         ],
-        [VMEM] * 7,
+        [SMEM] + [VMEM] * (6 + replicas),
         6 * slots * hidden_width * width,
         6 * hidden_width * width,
-    )(out_grad, down, gate_factor, up_factor, hidden, bundles, up_full)
+    )(my_replica, out_grad, down, gate_factor, up_factor, hidden, bundles, *blocks)
     returned = exchange(returned.reshape(experts, capacity, width + LANES))
     returned = returned.reshape(slots, width + LANES)
 
     node_error = jnp.sum(jnp.where(is_me, errors.reshape(experts, nodes), 0.0), axis=0)
     node_mean = node_error + lambda_targets[0]
     token_error = jnp.sum(in_node * node_error[None, :], axis=1)
-    at_slot = slot_row.reshape(tok_rows, 1) == jnp.arange(slots, dtype=I32)[None, :]
-    route_rows = jnp.dot(at_slot.astype(BF16), returned, preferred_element_type=F32)
-    value_grad = (above_grad.astype(F32) + token_error[:, None] * value_row).astype(BF16)
-    token_grad = (value_grad.astype(F32) + route_rows[:, :width]).astype(BF16)
-    gate_grad = (route_rows[:, width : width + 1] + route_rows[:, width + 1 : width + 2]) / gates
-    return token_grad, gate_grad, down_grad.astype(F32)[None], node_mean[None, :]
+    token_grad, gate_grad, down_out = call(
+        finish_body,
+        [
+            shape(tokens.shape, BF16),
+            shape(gates.shape, F32),
+            shape(down_grad.shape, F32),
+        ],
+        [VMEM] * 7,
+        2 * slots * tok_rows * width,
+        8 * slots * width,
+    )(returned, slot_row, above_grad, value_row, token_error[:, None], gates, down_grad)
+    return token_grad, gate_grad, down_out[None], node_mean[None, :]
 
 
 def solution(mesh):

time: 197 us -> 194 us (0.985)
  local copies, waits for them, and re-layouts: 8.71 us -> 12.1 us
  other arithmetic: 6.23 us -> 3.16 us
  waiting for transfers between devices: 60.6 us -> 58.6 us
    pallas_call x2, Pallas kernels: 7.72 us -> 4.83 us  [the longest x1 3.02 us: local(): call(finish_body, [shape(tokens.shape, BF16), shape(gates.shape, F32), sh...]
    pallas_call x1, Pallas kernels: 6.19 us -> 8.73 us  [local(): call(functools.partial(forward_body, replicas, capacity), [shape((slots,...]
    ppermute x8, waiting for transfers between devices: 32.5 us -> 30.5 us  [shift(): lax.ppermute(block, 'replica', [(i, (i + step) % count) for i in range(co...]
    unnamed x37 -> x27, local copies, waits for them, and re-layouts: 4.59 us -> 5.74 us
  transfers between devices with their start and end apart: 13 -> 13, of which waited for: 5 -> 6; matrix products, arithmetic and copies ran while one was open for 6% -> 6% of each run, Pallas kernels for 16% -> 14%
where the time goes in v3:
time: 194 us; the launch traced here: 193 us
  waiting for transfers between devices  58.6 us (30%)
  starting transfers between devices  47.9 us (25%)
  Pallas kernels  33.2 us (17%)
  blocking collectives  24.2 us (12%)
  between operations  14 us (7%)
  local copies, waits for them, and re-layouts  12.1 us (6%)
  other arithmetic  3.16 us (2%)
    ppermute x8, waiting for transfers between devices, shift(): lax.ppermute(block, 'replica', [(i, (i + step) % count) for i in range(co...  30.5 us
    all_to_all x2, waiting for transfers between devices, exchange(): lax.all_to_all(rows, 'expert', split_axis=0, concat_axis=0, tiled=True)  27.4 us
    ppermute x8, starting transfers between devices, shift(): lax.ppermute(block, 'replica', [(i, (i + step) % count) for i in range(co...  27.3 us
    all_to_all x1, blocking collectives, exchange(): lax.all_to_all(rows, 'expert', split_axis=0, concat_axis=0, tiled=True)  24.2 us
    all_to_all x2, starting transfers between devices, exchange(): lax.all_to_all(rows, 'expert', split_axis=0, concat_axis=0, tiled=True)  20.5 us
    pallas_call x1, Pallas kernels, local(): call(functools.partial(backward_body, replicas), [shape((slots, width + L...  8.76 us
    pallas_call x1, Pallas kernels, local(): call(functools.partial(forward_body, replicas, capacity), [shape((slots,...  8.73 us
    unnamed x27, local copies, waits for them, and re-layouts  5.74 us
  transfers between devices with their start and end apart: 13, of which 6 were waited for; matrix products, arithmetic and copies ran while one was open for 6% of the time, Pallas kernels for 14%

profile of v3, /device:TPU:1, one launch (start us, length us, event | category | flops | bytes accessed | tf_op | source)
XLA Modules:
  0.0 193.2 jit_solution(12193442094853415969)
XLA Ops:
  7.2 2.3 %shard_map.130 = bf16[272,768]{1,0:T(8,128)(2,1)} custom-call(s32[1]{0:T(128)} %bitcast.me, bf16[256,768]{1,0:T(8,128)(2,1)} %bitcast.35, bf16[96,2048]{1,0:T(8,128)(2,1)} %bitcast.34, f32[1,2048]{1,0:T(1,128)} %bitcast.37), custom_call_target="tpu_custom_call" | custom-call | bytes 786432 | tf_op jit(solution)/shard_map/pallas_call | solution.py:238
  10.3 4.0 %collective-permute-start = (bf16[256,768]{1,0:T(8,128)(2,1)}, bf16[256,768]{1,0:T(8,128)(2,1)S(1)}, u32[]{:S(2)}, u32[]{:S(2)}) collective-permute-start(bf16[256,768]{1,0:T(8,128)(2,1)} %bitcast.30), channel_id=1, source_target_pairs={{0,1},{1,2},{2,3},{3,4},{4,5},{5,6},{6,7},{7,0},{8,9},{9,10},{10,1... | collective-permute-start | bytes 1179656 | tf_op jit(solution)/shard_map/ppermute | solution.py:28
  14.3 3.8 %collective-permute-start.1 = (bf16[256,768]{1,0:T(8,128)(2,1)}, bf16[256,768]{1,0:T(8,128)(2,1)S(1)}, u32[]{:S(2)}, u32[]{:S(2)}) collective-permute-start(bf16[256,768]{1,0:T(8,128)(2,1)} %bitcast.31), channel_id=1, source_target_pairs={{0,7},{1,0},{2,1},{3,2},{4,3},{5,4},{6,5},{7,6},{8,15},{9,8},{10,9... | collective-permute-start | bytes 1179656 | tf_op jit(solution)/shard_map/ppermute | solution.py:28
  20.9 4.1 %shard_map.129 = (bf16[512,2176]{1,0:T(8,128)(2,1)}, s32[1,128]{1,0:T(1,128)}) custom-call(s32[1,128]{1,0:T(1,128)} %bitcast.43, f32[128,1]{1,0:T(8,128)} %copy.29.gates, s32[128,1]{1,0:T(8,128)} %copy.30.nodes, bf16[128,2048]{1,0:T(8,128)(2,1)} %tokens.1, bf16[128,2048]{1,0:T(8,128)(2,1)} %above.3), custom_call_target="tpu_custom_call" | custom-call | flops 268435456 | bytes 4194304 | tf_op jit(solution)/shard_map/pallas_call | solution.py:262
  25.1 14.4 %all-to-all-start = ((bf16[64,8,2176]{2,1,0:T(8,128)(2,1)}), bf16[64,8,2176]{2,1,0:T(8,128)(2,1)S(1)}, u32[]{:S(2)}, u32[]{:S(2)}) async-start(bf16[64,8,2176]{2,1,0:T(8,128)(2,1)} %bitcast.29), calls=%async_computation | async-start | bytes 4456448 | tf_op jit(solution)/shard_map/all_to_all | solution.py:23
  39.6 1.9 collective-permute-start.2
  41.5 4.6 %collective-permute-start.3 = (bf16[256,768]{1,0:T(8,128)(2,1)S(1)}, bf16[256,768]{1,0:T(8,128)(2,1)}, u32[]{:S(2)}, u32[]{:S(2)}) collective-permute-start(bf16[256,768]{1,0:T(8,128)(2,1)S(1)} %collective-permute-done.1.rest_2_), channel_id=1, source_target_pairs={{0,7},{1,0},{2,1},{3,2},{4,3},{5,4},{6,5},{7,6},{8,15},{9,8},{10,9... | collective-permute-start | bytes 1179656 | tf_op jit(solution)/shard_map/ppermute | solution.py:28
  46.1 15.9 %collective-permute-done.2.rest_3_ = bf16[256,768]{1,0:T(8,128)(2,1)} collective-permute-done((bf16[256,768]{1,0:T(8,128)(2,1)S(1)}, bf16[256,768]{1,0:T(8,128)(2,1)}, u32[]{:S(2)}, u32[]{:S(2)}) %collective-permute-start.2) | collective-permute-done | bytes 393248 | tf_op jit(solution)/shard_map/ppermute | solution.py:28
  62.0 1.9 collective-permute-start.4
  64.0 4.6 %collective-permute-start.5 = (bf16[256,768]{1,0:T(8,128)(2,1)}, bf16[256,768]{1,0:T(8,128)(2,1)S(1)}, u32[]{:S(2)}, u32[]{:S(2)}) collective-permute-start(bf16[256,768]{1,0:T(8,128)(2,1)} %collective-permute-done.3.rest_4_), channel_id=1, source_target_pairs={{0,7},{1,0},{2,1},{3,2},{4,3},{5,4},{6,5},{7,6},{8,15},{9,8},{10,9... | collective-permute-start | bytes 1179656 | tf_op jit(solution)/shard_map/ppermute | solution.py:28
  68.9 12.3 %collective-permute-done.4.rest_5_ = bf16[256,768]{1,0:T(8,128)(2,1)S(1)} collective-permute-done((bf16[256,768]{1,0:T(8,128)(2,1)}, bf16[256,768]{1,0:T(8,128)(2,1)S(1)}, u32[]{:S(2)}, u32[]{:S(2)}) %collective-permute-start.4) | collective-permute-done | bytes 393248 | tf_op jit(solution)/shard_map/ppermute | solution.py:28
  81.3 1.9 collective-permute-start.6
  83.2 4.6 %collective-permute-start.7 = (bf16[128,768]{1,0:T(8,128)(2,1)S(1)}, bf16[128,768]{1,0:T(8,128)(2,1)S(1)}, u32[]{:S(2)}, u32[]{:S(2)}) collective-permute-start(bf16[128,768]{1,0:T(8,128)(2,1)S(1)} %slice.9), channel_id=1, source_target_pairs={{0,7},{1,0},{2,1},{3,2},{4,3},{5,4},{6,5},{7,6},{8,15},{9,8},{10,9... | collective-permute-start | bytes 589832 | tf_op jit(solution)/shard_map/ppermute | solution.py:28
  91.4 1.8 shard_map.131.rest_7_
  93.4 1.4 copy-done
  94.8 8.7 %shard_map.132 = (bf16[256,2048]{1,0:T(8,128)(2,1)}, bf16[256,768]{1,0:T(8,128)(2,1)}, bf16[256,768]{1,0:T(8,128)(2,1)}, bf16[256,768]{1,0:T(8,128)(2,1)}, f32[2...) custom-call(s32[1]{0:T(128)} %bitcast.me, bf16[512,2176]{1,0:T(8,128)(2,1)} %bitcast.27, ...), custom_call_target="tpu_custom_call" | custom-call | flops 1610612736 | bytes 6291456 | tf_op jit(solution)/shard_map/pallas_call | solution.py:272
  104.6 24.2 %all_to_all.18 = f32[64,1,1024]{2,1,0:T(1,128)S(1)} all-to-all(f32[64,1,1024]{2,1,0:T(1,128)S(1)} %broadcast_in_dim.58), channel_id=1, replica_groups=mesh['expert'=64,'replica'=8] {'expert'}, dimensions={0} | all-to-all | bytes 524288 | tf_op jit(solution)/shard_map/all_to_all | solution.py:23
  129.5 4.5 %shard_map.133 = (bf16[256,2048]{1,0:T(8,128)(2,1)}, bf16[768,2048]{1,0:T(8,128)(2,1)}, f32[1,1024]{1,0:T(1,128)}) custom-call(f32[64,1024]{1,0:T(8,128)} %bitcast.36, f32[256,128]{1,0:T(8,128)} %get-tuple-element.21.notes, bf16[256,2048]{1,0:T(8,128)(2,1)} %get-tuple-element.22.above, f32[1,2048]{1,0:T(1,128)} %bitcast.38, ...), custom_call_target="tpu_custom_call" | custom-call | flops 805306368 | bytes 6291456 | tf_op jit(solution)/shard_map/pallas_call | solution.py:300
  134.1 8.8 %shard_map.134 = (bf16[256,2176]{1,0:T(8,128)(2,1)}, bf16[256,768]{1,0:T(8,128)(2,1)}, bf16[256,768]{1,0:T(8,128)(2,1)}) custom-call(s32[1]{0:T(128)} %bitcast.me, bf16[256,2048]{1,0:T(8,128)(2,1)} %get-tuple-element.24.grad, bf16[768,2048]{1,0:T(8,128)(2,1)} %bitcast.28, bf16[256,768]{1,0:T(8,128)(2,1)} %get-tuple-element.25.gate_factor, ...), custom_call_target="tpu_custom_call" | custom-call | flops 2415919104 | bytes 9437184 | tf_op jit(solution)/shard_map/pallas_call | solution.py:313
  142.9 2.2 %reshape.72 = bf16[64,4,2176]{2,1,0:T(4,128)(2,1)} reshape(bf16[256,2176]{1,0:T(8,128)(2,1)} %get-tuple-element.27) | data formatting | bytes 2228224 | tf_op jit(solution)/shard_map/reshape | solution.py:324
  145.1 6.0 %all-to-all-start.2 = ((bf16[64,4,2176]{2,1,0:T(4,128)(2,1)}), bf16[64,4,2176]{2,1,0:T(4,128)(2,1)S(1)}, u32[]{:S(2)}, u32[]{:S(2)}) async-start(bf16[64,4,2176]{2,1,0:T(4,128)(2,1)} %reshape.72), calls=%async_computation.2 | async-start | bytes 2228224 | tf_op jit(solution)/shard_map/all_to_all | solution.py:23
  153.8 27.3 %all-to-all-done.2 = bf16[64,4,2176]{2,1,0:T(4,128)(2,1)S(1)} async-done(((bf16[64,4,2176]{2,1,0:T(4,128)(2,1)}), bf16[64,4,2176]{2,1,0:T(4,128)(2,1)S(1)}, u32[]{:S(2)}, u32[]{:S(2)}) %all-to-all-start.2) | async-done | bytes 1114144 | tf_op jit(solution)/shard_map/all_to_all | solution.py:23
  182.2 3.0 %shard_map.135 = (bf16[128,2048]{1,0:T(8,128)(2,1)}, f32[128,1]{1,0:T(8,128)}, f32[96,2048]{1,0:T(8,128)}) custom-call(bf16[256,2176]{1,0:T(8,128)(2,1)} %reshape.73.returned, s32[1,128]{1,0:T(1,128)} %get-tuple-element.28.slot, bf16[128,2048]{1,0:T(8,128)(2,1)} %above.3, f32[1,2048]{1,0:T(1,128)} %bitcast.39, f32[128,1]{1,0:T(8,128)} %copy.31.error, ...), custom_call_target="tpu_custom_call" | custom-call | flops 134217728 | bytes 4194304 | tf_op jit(solution)/shard_map/pallas_call | solution.py:330
  185.2 1.4 copy.33
  (59 shorter events, 13.4 us)
Async XLA Ops:
  7.2 86.2 %all-gather.5.cloned.1.call-start = ((), (), s32[]{:S(2)}) async-start(), calls=%async_computation.5 | async-start | bytes 3760128 | tf_op jit(solution)/shard_map/all_gather | solution.py:245
  9.5 124.6 %all-gather.7.cloned.1.call-start = ((), (), s32[]{:S(2)}) async-start(), calls=%async_computation.6 | async-start | bytes 3538944 | tf_op jit(solution)/shard_map/all_gather | solution.py:287
  10.3 29.3 %collective-permute-start = (bf16[256,768]{1,0:T(8,128)(2,1)}, bf16[256,768]{1,0:T(8,128)(2,1)S(1)}, u32[]{:S(2)}, u32[]{:S(2)}) collective-permute-start(bf16[256,768]{1,0:T(8,128)(2,1)} %bitcast.30), channel_id=1, source_target_pairs={{0,1},{1,2},{2,3},{3,4},{4,5},{5,6},{6,7},{7,0},{8,9},{9,10},{10,1... | collective-permute-start | bytes 1179656 | tf_op jit(solution)/shard_map/ppermute | solution.py:28
  14.3 27.2 %collective-permute-start.1 = (bf16[256,768]{1,0:T(8,128)(2,1)}, bf16[256,768]{1,0:T(8,128)(2,1)S(1)}, u32[]{:S(2)}, u32[]{:S(2)}) collective-permute-start(bf16[256,768]{1,0:T(8,128)(2,1)} %bitcast.31), channel_id=1, source_target_pairs={{0,7},{1,0},{2,1},{3,2},{4,3},{5,4},{6,5},{7,6},{8,15},{9,8},{10,9... | collective-permute-start | bytes 1179656 | tf_op jit(solution)/shard_map/ppermute | solution.py:28
  25.1 43.5 %copy-start.3 = (bf16[128,2048]{1,0:T(8,128)(2,1)S(1)}, bf16[128,2048]{1,0:T(8,128)(2,1)}, u32[]{:S(2)}) copy-start(bf16[128,2048]{1,0:T(8,128)(2,1)} %tokens.1) | copy-start | bytes 1572868
  25.1 43.5 %copy-start.6 = (f32[2048]{0:T(1024)S(1)}, f32[2048]{0:T(1024)}, u32[]{:S(2)}) copy-start(f32[2048]{0:T(1024)} %param.14) | copy-start | bytes 24580
  25.1 43.7 %copy-start.8 = (s32[1,128]{1,0:T(1,128)S(1)}, s32[1,128]{1,0:T(1,128)}, u32[]{:S(2)}) copy-start(s32[1,128]{1,0:T(1,128)} %param.17) | copy-start | bytes 1540
  25.1 68.3 %all-to-all-start = ((bf16[64,8,2176]{2,1,0:T(8,128)(2,1)}), bf16[64,8,2176]{2,1,0:T(8,128)(2,1)S(1)}, u32[]{:S(2)}, u32[]{:S(2)}) async-start(bf16[64,8,2176]{2,1,0:T(8,128)(2,1)} %bitcast.29), calls=%async_computation | async-start | bytes 4456448 | tf_op jit(solution)/shard_map/all_to_all | solution.py:23
  39.5 142.7 %reduce-scatter.2.cloned.1.call-start = ((), (), s32[]{:S(2)}) async-start(), calls=%async_computation.4 | async-start | bytes 3538944 | tf_op jit(solution)/shard_map/reduce_scatter | solution.py:311
  39.6 6.5 %copy-start.4 = (bf16[256,768]{1,0:T(8,128)(2,1)}, bf16[256,768]{1,0:T(8,128)(2,1)S(1)}, u32[]{:S(2)}) copy-start(bf16[256,768]{1,0:T(8,128)(2,1)S(1)} %collective-permute-done.rest_1_) | copy-start | bytes 1179652
  39.6 22.4 %collective-permute-start.2 = (bf16[256,768]{1,0:T(8,128)(2,1)S(1)}, bf16[256,768]{1,0:T(8,128)(2,1)}, u32[]{:S(2)}, u32[]{:S(2)}) collective-permute-start(bf16[256,768]{1,0:T(8,128)(2,1)S(1)} %collective-permute-done.rest_1_), channel_id=1, source_target_pairs={{0,1},{1,2},{2,3},{3,4},{4,5},{5,6},{6,7},{7,0},{8,9},{9,10},{10,1... | collective-permute-start | bytes 1179656 | tf_op jit(solution)/shard_map/ppermute | solution.py:28
  41.5 22.4 %copy-start.5 = (bf16[256,768]{1,0:T(8,128)(2,1)}, bf16[256,768]{1,0:T(8,128)(2,1)S(1)}, u32[]{:S(2)}) copy-start(bf16[256,768]{1,0:T(8,128)(2,1)S(1)} %collective-permute-done.1.rest_2_) | copy-start | bytes 1179652
  41.5 22.4 %collective-permute-start.3 = (bf16[256,768]{1,0:T(8,128)(2,1)S(1)}, bf16[256,768]{1,0:T(8,128)(2,1)}, u32[]{:S(2)}, u32[]{:S(2)}) collective-permute-start(bf16[256,768]{1,0:T(8,128)(2,1)S(1)} %collective-permute-done.1.rest_2_), channel_id=1, source_target_pairs={{0,7},{1,0},{2,1},{3,2},{4,3},{5,4},{6,5},{7,6},{8,15},{9,8},{10,9... | collective-permute-start | bytes 1179656 | tf_op jit(solution)/shard_map/ppermute | solution.py:28
  62.0 19.2 %collective-permute-start.4 = (bf16[256,768]{1,0:T(8,128)(2,1)}, bf16[256,768]{1,0:T(8,128)(2,1)S(1)}, u32[]{:S(2)}, u32[]{:S(2)}) collective-permute-start(bf16[256,768]{1,0:T(8,128)(2,1)} %collective-permute-done.2.rest_3_), channel_id=1, source_target_pairs={{0,1},{1,2},{2,3},{3,4},{4,5},{5,6},{6,7},{7,0},{8,9},{9,10},{10,1... | collective-permute-start | bytes 1179656 | tf_op jit(solution)/shard_map/ppermute | solution.py:28
  64.0 19.2 %collective-permute-start.5 = (bf16[256,768]{1,0:T(8,128)(2,1)}, bf16[256,768]{1,0:T(8,128)(2,1)S(1)}, u32[]{:S(2)}, u32[]{:S(2)}) collective-permute-start(bf16[256,768]{1,0:T(8,128)(2,1)} %collective-permute-done.3.rest_4_), channel_id=1, source_target_pairs={{0,7},{1,0},{2,1},{3,2},{4,3},{5,4},{6,5},{7,6},{8,15},{9,8},{10,9... | collective-permute-start | bytes 1179656 | tf_op jit(solution)/shard_map/ppermute | solution.py:28
  81.2 12.0 %copy-start.1 = (bf16[256,768]{1,0:T(8,128)(2,1)}, bf16[256,768]{1,0:T(8,128)(2,1)S(1)}, u32[]{:S(2)}) copy-start(bf16[256,768]{1,0:T(8,128)(2,1)S(1)} %collective-permute-done.4.rest_5_) | copy-start | bytes 1179652
  81.3 8.5 %collective-permute-start.6 = (bf16[128,768]{1,0:T(8,128)(2,1)S(1)}, bf16[128,768]{1,0:T(8,128)(2,1)S(1)}, u32[]{:S(2)}, u32[]{:S(2)}) collective-permute-start(bf16[128,768]{1,0:T(8,128)(2,1)S(1)} %slice.8), channel_id=1, source_target_pairs={{0,1},{1,2},{2,3},{3,4},{4,5},{5,6},{6,7},{7,0},{8,9},{9,10},{10,1... | collective-permute-start | bytes 589832 | tf_op jit(solution)/shard_map/ppermute | solution.py:28
  83.2 10.0 %copy-start.2 = (bf16[256,768]{1,0:T(8,128)(2,1)}, bf16[256,768]{1,0:T(8,128)(2,1)S(1)}, u32[]{:S(2)}) copy-start(bf16[256,768]{1,0:T(8,128)(2,1)S(1)} %collective-permute-done.5.rest_6_) | copy-start | bytes 1179652
  83.2 7.5 %collective-permute-start.7 = (bf16[128,768]{1,0:T(8,128)(2,1)S(1)}, bf16[128,768]{1,0:T(8,128)(2,1)S(1)}, u32[]{:S(2)}, u32[]{:S(2)}) collective-permute-start(bf16[128,768]{1,0:T(8,128)(2,1)S(1)} %slice.9), channel_id=1, source_target_pairs={{0,7},{1,0},{2,1},{3,2},{4,3},{5,4},{6,5},{7,6},{8,15},{9,8},{10,9... | collective-permute-start | bytes 589832 | tf_op jit(solution)/shard_map/ppermute | solution.py:28
  89.8 0.9 copy-start.10
  93.4 1.4 copy-start
  142.8 8.8 %copy-start.7 = (f32[1,1024]{1,0:T(1,128)S(1)}, f32[1,1024]{1,0:T(1,128)}, u32[]{:S(2)}) copy-start(f32[1,1024]{1,0:T(1,128)} %get-tuple-element.29) | copy-start | bytes 12292
  142.9 10.4 %copy-start.9 = (f32[1,16]{1,0:T(1,128)S(1)}, f32[1,16]{1,0:T(1,128)}, u32[]{:S(2)}) copy-start(f32[1,16]{1,0:T(1,128)} %param.18) | copy-start | bytes 196
  145.1 36.0 %all-to-all-start.2 = ((bf16[64,4,2176]{2,1,0:T(4,128)(2,1)}), bf16[64,4,2176]{2,1,0:T(4,128)(2,1)S(1)}, u32[]{:S(2)}, u32[]{:S(2)}) async-start(bf16[64,4,2176]{2,1,0:T(4,128)(2,1)} %reshape.72), calls=%async_computation.2 | async-start | bytes 2228224 | tf_op jit(solution)/shard_map/all_to_all | solution.py:23
  (1 other events, 0.7 us)
Sparse Core Ops, SparseCore 0:
  10.7 67.6 all-gather.4
  80.4 47.4 all-gather.6
  134.2 42.5 reduce-scatter.1

commit v4 on v3

--- a/solution.py
+++ b/solution.py
@@ -59,20 +59,18 @@
     chosen = chosen + jnp.dot(pick_above, above[...], preferred_element_type=F32)
     out[:, :width] = chosen.astype(BF16)
     gate = gates[...]
-    high = gate.astype(BF16)
-    rest = gate - high.astype(F32)
-    middle = rest.astype(BF16)
-    low = (rest - middle.astype(F32)).astype(BF16)
+    high = gate.astype(BF16).astype(F32)
+    middle = (gate - high).astype(BF16).astype(F32)
+    low = gate - high - middle
     node = nodes[...]
-    same = (iota((rows, 16), 1) == node).astype(F32)
-    count = jnp.sum(same * jnp.sum(same, axis=0, keepdims=True), axis=1, keepdims=True)
-    lane = iota((rows, LANES), 1)
-    notes = jnp.where(lane == 0, high.astype(F32), 0.0)
-    notes = jnp.where(lane == 1, middle.astype(F32), notes)
-    notes = jnp.where(lane == 2, low.astype(F32), notes)
-    notes = jnp.where(lane == 3, node.astype(F32), notes)
-    notes = jnp.where(lane == 4, count, notes).astype(BF16)
-    out[:, width:] = jnp.dot(pick, notes, preferred_element_type=F32).astype(BF16)
+    same = (iota((16, rows), 0) == node).astype(F32)
+    count = jnp.sum(same * jnp.sum(same, axis=1, keepdims=True), axis=0, keepdims=True)
+    lane = iota((LANES, rows), 0)
+    notes = jnp.where(lane == 0, high, jnp.where(lane == 1, middle, jnp.where(lane == 2, low, 0.0)))
+    notes = jnp.where(lane == 3, node.astype(F32), jnp.where(lane == 4, count, notes))
+    out[:, width:] = lax.dot_general(
+        pick, notes.astype(BF16), NT, preferred_element_type=F32
+    ).astype(BF16)
 
 
 def bundle_body(me, gate, down, value_weight, out):
@@ -204,10 +202,11 @@
     slots = returned.shape[0]
     rows, width = above.shape
     pick = (iota((slots, rows), 0) == slot[...]).astype(BF16)
-    mine = lax.dot_general(pick, returned[...], TN, preferred_element_type=F32)
+    mine = lax.dot_general(pick, returned[:, :width], TN, preferred_element_type=F32)
     grad = (above[...].astype(F32) + error[...] * value_weight[...]).astype(BF16)
-    token_out[...] = (grad.astype(F32) + mine[:, :width]).astype(BF16)
-    gate_out[...] = (mine[:, width : width + 1] + mine[:, width + 1 : width + 2]) / gates[...]
+    token_out[...] = (grad.astype(F32) + mine).astype(BF16)
+    tail = lax.dot_general(returned[:, width:], pick, TN, preferred_element_type=F32)
+    gate_out[...] = (tail[0:1, :] + tail[1:2, :]) / gates[...]
     down_out[...] = sums[...].astype(F32)
 
 
@@ -232,6 +231,7 @@
     nodes = lambda_targets.shape[1]
     shape = jax.ShapeDtypeStruct
     value_row = value_weight[None, :]
+    gate_row = gates.reshape(1, tok_rows)
     me = lax.axis_index("expert")
     my_replica = lax.axis_index("replica").astype(I32).reshape(1)
 
@@ -265,7 +265,7 @@
         [VMEM] * 5,
         4 * slots * tok_rows * width,
         8 * slots * width,
-    )(routes.reshape(1, tok_rows), gates, node_ids.reshape(tok_rows, 1), tokens, above_grad)
+    )(routes.reshape(1, tok_rows), gate_row, node_ids, tokens, above_grad)
     both = exchange(both.reshape(experts, 2 * capacity, width + LANES))
     both = both.reshape(2 * slots, width + LANES)
 
@@ -331,14 +331,14 @@
         finish_body,
         [
             shape(tokens.shape, BF16),
-            shape(gates.shape, F32),
+            shape(gate_row.shape, F32),
             shape(down_grad.shape, F32),
         ],
         [VMEM] * 7,
         2 * slots * tok_rows * width,
         8 * slots * width,
-    )(returned, slot_row, above_grad, value_row, token_error[:, None], gates, down_grad)
-    return token_grad, gate_grad, down_out[None], node_mean[None, :]
+    )(returned, slot_row, above_grad, value_row, token_error[:, None], gate_row, down_grad)
+    return token_grad, gate_grad.reshape(gates.shape), down_out[None], node_mean[None, :]
 
 
 def solution(mesh):

time: 194 us -> 194 us (level)
  local copies, waits for them, and re-layouts: 12.1 us -> 7.82 us
  waiting for transfers between devices: 58.6 us -> 61.6 us
    ppermute x8, waiting for transfers between devices: 30.5 us -> 33.5 us  [shift(): lax.ppermute(block, 'replica', [(i, (i + step) % count) for i in range(co...]
    unnamed x27 -> x25, local copies, waits for them, and re-layouts: 5.74 us -> 2.89 us
  transfers between devices with their start and end apart: 13 -> 13, of which waited for: 6 -> 5; matrix products, arithmetic and copies ran while one was open for 6% -> 5% of each run, Pallas kernels for 14% -> 14%
where the time goes in v4:
time: 194 us; the launch traced here: 193 us
  waiting for transfers between devices  61.6 us (32%)
  starting transfers between devices  49.4 us (25%)
  Pallas kernels  33.3 us (17%)
  blocking collectives  24.1 us (12%)
  between operations  14 us (7%)
  local copies, waits for them, and re-layouts  7.82 us (4%)
  other arithmetic  3.16 us (2%)
    ppermute x8, waiting for transfers between devices, shift(): lax.ppermute(block, 'replica', [(i, (i + step) % count) for i in range(co...  33.5 us
    ppermute x8, starting transfers between devices, shift(): lax.ppermute(block, 'replica', [(i, (i + step) % count) for i in range(co...  27.3 us
    all_to_all x2, waiting for transfers between devices, exchange(): lax.all_to_all(rows, 'expert', split_axis=0, concat_axis=0, tiled=True)  27.3 us
    all_to_all x1, blocking collectives, exchange(): lax.all_to_all(rows, 'expert', split_axis=0, concat_axis=0, tiled=True)  24.1 us
    all_to_all x2, starting transfers between devices, exchange(): lax.all_to_all(rows, 'expert', split_axis=0, concat_axis=0, tiled=True)  21.9 us
    pallas_call x1, Pallas kernels, local(): call(functools.partial(forward_body, replicas, capacity), [shape((slots,...  8.82 us
    pallas_call x1, Pallas kernels, local(): call(functools.partial(backward_body, replicas), [shape((slots, width + L...  8.76 us
    pallas_call x1, Pallas kernels, local(): call(functools.partial(partial_body, capacity), [shape((slots, width), BF...  4.51 us
  transfers between devices with their start and end apart: 13, of which 5 were waited for; matrix products, arithmetic and copies ran while one was open for 5% of the time, Pallas kernels for 14%

profile of v4, /device:TPU:1, one launch (start us, length us, event | category | flops | bytes accessed | tf_op | source)
XLA Modules:
  0.0 193.3 jit_solution(5333523558652069101)
XLA Ops:
  7.2 2.3 %shard_map.130 = bf16[272,768]{1,0:T(8,128)(2,1)} custom-call(s32[1]{0:T(128)} %bitcast.me, bf16[256,768]{1,0:T(8,128)(2,1)} %bitcast.36, bf16[96,2048]{1,0:T(8,128)(2,1)} %bitcast.35, f32[1,2048]{1,0:T(1,128)} %bitcast.38), custom_call_target="tpu_custom_call" | custom-call | bytes 786432 | tf_op jit(solution)/shard_map/pallas_call | solution.py:238
  10.3 4.0 %collective-permute-start = (bf16[256,768]{1,0:T(8,128)(2,1)}, bf16[256,768]{1,0:T(8,128)(2,1)S(1)}, u32[]{:S(2)}, u32[]{:S(2)}) collective-permute-start(bf16[256,768]{1,0:T(8,128)(2,1)} %bitcast.31), channel_id=1, source_target_pairs={{0,1},{1,2},{2,3},{3,4},{4,5},{5,6},{6,7},{7,0},{8,9},{9,10},{10,1... | collective-permute-start | bytes 1179656 | tf_op jit(solution)/shard_map/ppermute | solution.py:28
  14.3 3.8 %collective-permute-start.1 = (bf16[256,768]{1,0:T(8,128)(2,1)}, bf16[256,768]{1,0:T(8,128)(2,1)S(1)}, u32[]{:S(2)}, u32[]{:S(2)}) collective-permute-start(bf16[256,768]{1,0:T(8,128)(2,1)} %bitcast.32), channel_id=1, source_target_pairs={{0,7},{1,0},{2,1},{3,2},{4,3},{5,4},{6,5},{7,6},{8,15},{9,8},{10,9... | collective-permute-start | bytes 1179656 | tf_op jit(solution)/shard_map/ppermute | solution.py:28
  18.1 4.1 %shard_map.129 = (bf16[512,2176]{1,0:T(8,128)(2,1)}, s32[1,128]{1,0:T(1,128)}) custom-call(s32[1,128]{1,0:T(1,128)} %bitcast.45, f32[1,128]{1,0:T(1,128)} %bitcast.43, s32[1,128]{1,0:T(1,128)} %nodes.1, bf16[128,2048]{1,0:T(8,128)(2,1)} %tokens.1, bf16[128,2048]{1,0:T(8,128)(2,1)} %above.3), custom_call_target="tpu_custom_call" | custom-call | flops 268435456 | bytes 4194304 | tf_op jit(solution)/shard_map/pallas_call | solution.py:262
  22.3 14.4 %all-to-all-start = ((bf16[64,8,2176]{2,1,0:T(8,128)(2,1)}), bf16[64,8,2176]{2,1,0:T(8,128)(2,1)S(1)}, u32[]{:S(2)}, u32[]{:S(2)}) async-start(bf16[64,8,2176]{2,1,0:T(8,128)(2,1)} %bitcast.30), calls=%async_computation | async-start | bytes 4456448 | tf_op jit(solution)/shard_map/all_to_all | solution.py:23
  36.8 1.9 collective-permute-start.2
  38.7 4.6 %collective-permute-start.3 = (bf16[256,768]{1,0:T(8,128)(2,1)S(1)}, bf16[256,768]{1,0:T(8,128)(2,1)}, u32[]{:S(2)}, u32[]{:S(2)}) collective-permute-start(bf16[256,768]{1,0:T(8,128)(2,1)S(1)} %collective-permute-done.1.rest_2_), channel_id=1, source_target_pairs={{0,7},{1,0},{2,1},{3,2},{4,3},{5,4},{6,5},{7,6},{8,15},{9,8},{10,9... | collective-permute-start | bytes 1179656 | tf_op jit(solution)/shard_map/ppermute | solution.py:28
  43.3 15.9 %collective-permute-done.2.rest_3_ = bf16[256,768]{1,0:T(8,128)(2,1)} collective-permute-done((bf16[256,768]{1,0:T(8,128)(2,1)S(1)}, bf16[256,768]{1,0:T(8,128)(2,1)}, u32[]{:S(2)}, u32[]{:S(2)}) %collective-permute-start.2) | collective-permute-done | bytes 393248 | tf_op jit(solution)/shard_map/ppermute | solution.py:28
  59.2 1.9 collective-permute-start.4
  61.1 4.6 %collective-permute-start.5 = (bf16[256,768]{1,0:T(8,128)(2,1)}, bf16[256,768]{1,0:T(8,128)(2,1)S(1)}, u32[]{:S(2)}, u32[]{:S(2)}) collective-permute-start(bf16[256,768]{1,0:T(8,128)(2,1)} %collective-permute-done.3.rest_4_), channel_id=1, source_target_pairs={{0,7},{1,0},{2,1},{3,2},{4,3},{5,4},{6,5},{7,6},{8,15},{9,8},{10,9... | collective-permute-start | bytes 1179656 | tf_op jit(solution)/shard_map/ppermute | solution.py:28
  66.1 15.3 %collective-permute-done.4.rest_5_ = bf16[256,768]{1,0:T(8,128)(2,1)S(1)} collective-permute-done((bf16[256,768]{1,0:T(8,128)(2,1)}, bf16[256,768]{1,0:T(8,128)(2,1)S(1)}, u32[]{:S(2)}, u32[]{:S(2)}) %collective-permute-start.4) | collective-permute-done | bytes 393248 | tf_op jit(solution)/shard_map/ppermute | solution.py:28
  81.4 1.9 collective-permute-start.6
  83.3 4.6 %collective-permute-start.7 = (bf16[128,768]{1,0:T(8,128)(2,1)S(1)}, bf16[128,768]{1,0:T(8,128)(2,1)S(1)}, u32[]{:S(2)}, u32[]{:S(2)}) collective-permute-start(bf16[128,768]{1,0:T(8,128)(2,1)S(1)} %slice.9), channel_id=1, source_target_pairs={{0,7},{1,0},{2,1},{3,2},{4,3},{5,4},{6,5},{7,6},{8,15},{9,8},{10,9... | collective-permute-start | bytes 589832 | tf_op jit(solution)/shard_map/ppermute | solution.py:28
  88.6 1.4 collective-permute-done.6.high
  91.6 1.8 shard_map.131.rest_7_
  93.5 1.4 copy-done
  94.9 8.8 %shard_map.132 = (bf16[256,2048]{1,0:T(8,128)(2,1)}, bf16[256,768]{1,0:T(8,128)(2,1)}, bf16[256,768]{1,0:T(8,128)(2,1)}, bf16[256,768]{1,0:T(8,128)(2,1)}, f32[2...) custom-call(s32[1]{0:T(128)} %bitcast.me, bf16[512,2176]{1,0:T(8,128)(2,1)} %bitcast.28, ...), custom_call_target="tpu_custom_call" | custom-call | flops 1610612736 | bytes 6291456 | tf_op jit(solution)/shard_map/pallas_call | solution.py:272
  104.8 24.1 %all_to_all.18 = f32[64,1,1024]{2,1,0:T(1,128)S(1)} all-to-all(f32[64,1,1024]{2,1,0:T(1,128)S(1)} %broadcast_in_dim.58), channel_id=1, replica_groups=mesh['expert'=64,'replica'=8] {'expert'}, dimensions={0} | all-to-all | bytes 524288 | tf_op jit(solution)/shard_map/all_to_all | solution.py:23
  129.6 4.5 %shard_map.133 = (bf16[256,2048]{1,0:T(8,128)(2,1)}, bf16[768,2048]{1,0:T(8,128)(2,1)}, f32[1,1024]{1,0:T(1,128)}) custom-call(f32[64,1024]{1,0:T(8,128)} %bitcast.37, f32[256,128]{1,0:T(8,128)} %get-tuple-element.21.notes, bf16[256,2048]{1,0:T(8,128)(2,1)} %get-tuple-element.22.above, f32[1,2048]{1,0:T(1,128)} %bitcast.39, ...), custom_call_target="tpu_custom_call" | custom-call | flops 805306368 | bytes 6291456 | tf_op jit(solution)/shard_map/pallas_call | solution.py:300
  134.2 8.8 %shard_map.134 = (bf16[256,2176]{1,0:T(8,128)(2,1)}, bf16[256,768]{1,0:T(8,128)(2,1)}, bf16[256,768]{1,0:T(8,128)(2,1)}) custom-call(s32[1]{0:T(128)} %bitcast.me, bf16[256,2048]{1,0:T(8,128)(2,1)} %get-tuple-element.24.grad, bf16[768,2048]{1,0:T(8,128)(2,1)} %bitcast.29, bf16[256,768]{1,0:T(8,128)(2,1)} %get-tuple-element.25.gate_factor, ...), custom_call_target="tpu_custom_call" | custom-call | flops 2415919104 | bytes 9437184 | tf_op jit(solution)/shard_map/pallas_call | solution.py:313
  142.9 2.2 %reshape.75 = bf16[64,4,2176]{2,1,0:T(4,128)(2,1)} reshape(bf16[256,2176]{1,0:T(8,128)(2,1)} %get-tuple-element.27) | data formatting | bytes 2228224 | tf_op jit(solution)/shard_map/reshape | solution.py:324
  145.1 7.5 %all-to-all-start.2 = ((bf16[64,4,2176]{2,1,0:T(4,128)(2,1)}), bf16[64,4,2176]{2,1,0:T(4,128)(2,1)S(1)}, u32[]{:S(2)}, u32[]{:S(2)}) async-start(bf16[64,4,2176]{2,1,0:T(4,128)(2,1)} %reshape.75), calls=%async_computation.2 | async-start | bytes 2228224 | tf_op jit(solution)/shard_map/all_to_all | solution.py:23
  155.3 27.3 %all-to-all-done.2 = bf16[64,4,2176]{2,1,0:T(4,128)(2,1)S(1)} async-done(((bf16[64,4,2176]{2,1,0:T(4,128)(2,1)}), bf16[64,4,2176]{2,1,0:T(4,128)(2,1)S(1)}, u32[]{:S(2)}, u32[]{:S(2)}) %all-to-all-start.2) | async-done | bytes 1114144 | tf_op jit(solution)/shard_map/all_to_all | solution.py:23
  183.7 3.0 %shard_map.135 = (bf16[128,2048]{1,0:T(8,128)(2,1)}, f32[1,128]{1,0:T(1,128)}, f32[96,2048]{1,0:T(8,128)}) custom-call(bf16[256,2176]{1,0:T(8,128)(2,1)} %reshape.76.returned, s32[1,128]{1,0:T(1,128)} %get-tuple-element.28.slot, bf16[128,2048]{1,0:T(8,128)(2,1)} %above.3, f32[1,2048]{1,0:T(1,128)} %bitcast.40, f32[128,1]{1,0:T(8,128)} %copy.17.error, ...), custom_call_target="tpu_custom_call" | custom-call | flops 134217728 | bytes 4194304 | tf_op jit(solution)/shard_map/pallas_call | solution.py:330
  (56 shorter events, 9.2 us)
Async XLA Ops:
  7.2 86.3 %all-gather.5.cloned.1.call-start = ((), (), s32[]{:S(2)}) async-start(), calls=%async_computation.5 | async-start | bytes 3760128 | tf_op jit(solution)/shard_map/all_gather | solution.py:245
  9.5 124.6 %all-gather.7.cloned.1.call-start = ((), (), s32[]{:S(2)}) async-start(), calls=%async_computation.6 | async-start | bytes 3538944 | tf_op jit(solution)/shard_map/all_gather | solution.py:287
  10.3 26.5 %collective-permute-start = (bf16[256,768]{1,0:T(8,128)(2,1)}, bf16[256,768]{1,0:T(8,128)(2,1)S(1)}, u32[]{:S(2)}, u32[]{:S(2)}) collective-permute-start(bf16[256,768]{1,0:T(8,128)(2,1)} %bitcast.31), channel_id=1, source_target_pairs={{0,1},{1,2},{2,3},{3,4},{4,5},{5,6},{6,7},{7,0},{8,9},{9,10},{10,1... | collective-permute-start | bytes 1179656 | tf_op jit(solution)/shard_map/ppermute | solution.py:28
  14.3 24.4 %collective-permute-start.1 = (bf16[256,768]{1,0:T(8,128)(2,1)}, bf16[256,768]{1,0:T(8,128)(2,1)S(1)}, u32[]{:S(2)}, u32[]{:S(2)}) collective-permute-start(bf16[256,768]{1,0:T(8,128)(2,1)} %bitcast.32), channel_id=1, source_target_pairs={{0,7},{1,0},{2,1},{3,2},{4,3},{5,4},{6,5},{7,6},{8,15},{9,8},{10,9... | collective-permute-start | bytes 1179656 | tf_op jit(solution)/shard_map/ppermute | solution.py:28
  22.3 43.5 %copy-start.3 = (bf16[128,2048]{1,0:T(8,128)(2,1)S(1)}, bf16[128,2048]{1,0:T(8,128)(2,1)}, u32[]{:S(2)}) copy-start(bf16[128,2048]{1,0:T(8,128)(2,1)} %tokens.1) | copy-start | bytes 1572868
  22.3 43.5 %copy-start.6 = (f32[2048]{0:T(1024)S(1)}, f32[2048]{0:T(1024)}, u32[]{:S(2)}) copy-start(f32[2048]{0:T(1024)} %param.14) | copy-start | bytes 24580
  22.3 43.7 %copy-start.8 = (s32[1,128]{1,0:T(1,128)S(1)}, s32[1,128]{1,0:T(1,128)}, u32[]{:S(2)}) copy-start(s32[1,128]{1,0:T(1,128)} %nodes.1) | copy-start | bytes 1540
  22.3 71.2 %all-to-all-start = ((bf16[64,8,2176]{2,1,0:T(8,128)(2,1)}), bf16[64,8,2176]{2,1,0:T(8,128)(2,1)S(1)}, u32[]{:S(2)}, u32[]{:S(2)}) async-start(bf16[64,8,2176]{2,1,0:T(8,128)(2,1)} %bitcast.30), calls=%async_computation | async-start | bytes 4456448 | tf_op jit(solution)/shard_map/all_to_all | solution.py:23
  36.7 147.0 %reduce-scatter.2.cloned.1.call-start = ((), (), s32[]{:S(2)}) async-start(), calls=%async_computation.4 | async-start | bytes 3538944 | tf_op jit(solution)/shard_map/reduce_scatter | solution.py:311
  36.8 6.5 %copy-start.4 = (bf16[256,768]{1,0:T(8,128)(2,1)}, bf16[256,768]{1,0:T(8,128)(2,1)S(1)}, u32[]{:S(2)}) copy-start(bf16[256,768]{1,0:T(8,128)(2,1)S(1)} %collective-permute-done.rest_1_) | copy-start | bytes 1179652
  36.8 22.4 %collective-permute-start.2 = (bf16[256,768]{1,0:T(8,128)(2,1)S(1)}, bf16[256,768]{1,0:T(8,128)(2,1)}, u32[]{:S(2)}, u32[]{:S(2)}) collective-permute-start(bf16[256,768]{1,0:T(8,128)(2,1)S(1)} %collective-permute-done.rest_1_), channel_id=1, source_target_pairs={{0,1},{1,2},{2,3},{3,4},{4,5},{5,6},{6,7},{7,0},{8,9},{9,10},{10,1... | collective-permute-start | bytes 1179656 | tf_op jit(solution)/shard_map/ppermute | solution.py:28
  38.7 22.4 %copy-start.5 = (bf16[256,768]{1,0:T(8,128)(2,1)}, bf16[256,768]{1,0:T(8,128)(2,1)S(1)}, u32[]{:S(2)}) copy-start(bf16[256,768]{1,0:T(8,128)(2,1)S(1)} %collective-permute-done.1.rest_2_) | copy-start | bytes 1179652
  38.7 22.4 %collective-permute-start.3 = (bf16[256,768]{1,0:T(8,128)(2,1)S(1)}, bf16[256,768]{1,0:T(8,128)(2,1)}, u32[]{:S(2)}, u32[]{:S(2)}) collective-permute-start(bf16[256,768]{1,0:T(8,128)(2,1)S(1)} %collective-permute-done.1.rest_2_), channel_id=1, source_target_pairs={{0,7},{1,0},{2,1},{3,2},{4,3},{5,4},{6,5},{7,6},{8,15},{9,8},{10,9... | collective-permute-start | bytes 1179656 | tf_op jit(solution)/shard_map/ppermute | solution.py:28
  59.2 22.1 %collective-permute-start.4 = (bf16[256,768]{1,0:T(8,128)(2,1)}, bf16[256,768]{1,0:T(8,128)(2,1)S(1)}, u32[]{:S(2)}, u32[]{:S(2)}) collective-permute-start(bf16[256,768]{1,0:T(8,128)(2,1)} %collective-permute-done.2.rest_3_), channel_id=1, source_target_pairs={{0,1},{1,2},{2,3},{3,4},{4,5},{5,6},{6,7},{7,0},{8,9},{9,10},{10,1... | collective-permute-start | bytes 1179656 | tf_op jit(solution)/shard_map/ppermute | solution.py:28
  61.1 22.1 %collective-permute-start.5 = (bf16[256,768]{1,0:T(8,128)(2,1)}, bf16[256,768]{1,0:T(8,128)(2,1)S(1)}, u32[]{:S(2)}, u32[]{:S(2)}) collective-permute-start(bf16[256,768]{1,0:T(8,128)(2,1)} %collective-permute-done.3.rest_4_), channel_id=1, source_target_pairs={{0,7},{1,0},{2,1},{3,2},{4,3},{5,4},{6,5},{7,6},{8,15},{9,8},{10,9... | collective-permute-start | bytes 1179656 | tf_op jit(solution)/shard_map/ppermute | solution.py:28
  81.3 12.1 %copy-start.1 = (bf16[256,768]{1,0:T(8,128)(2,1)}, bf16[256,768]{1,0:T(8,128)(2,1)S(1)}, u32[]{:S(2)}) copy-start(bf16[256,768]{1,0:T(8,128)(2,1)S(1)} %collective-permute-done.4.rest_5_) | copy-start | bytes 1179652
  81.4 8.6 %collective-permute-start.6 = (bf16[128,768]{1,0:T(8,128)(2,1)S(1)}, bf16[128,768]{1,0:T(8,128)(2,1)S(1)}, u32[]{:S(2)}, u32[]{:S(2)}) collective-permute-start(bf16[128,768]{1,0:T(8,128)(2,1)S(1)} %slice.8), channel_id=1, source_target_pairs={{0,1},{1,2},{2,3},{3,4},{4,5},{5,6},{6,7},{7,0},{8,9},{9,10},{10,1... | collective-permute-start | bytes 589832 | tf_op jit(solution)/shard_map/ppermute | solution.py:28
  83.3 10.1 %copy-start.2 = (bf16[256,768]{1,0:T(8,128)(2,1)}, bf16[256,768]{1,0:T(8,128)(2,1)S(1)}, u32[]{:S(2)}) copy-start(bf16[256,768]{1,0:T(8,128)(2,1)S(1)} %collective-permute-done.5.rest_6_) | copy-start | bytes 1179652
  83.3 7.6 %collective-permute-start.7 = (bf16[128,768]{1,0:T(8,128)(2,1)S(1)}, bf16[128,768]{1,0:T(8,128)(2,1)S(1)}, u32[]{:S(2)}, u32[]{:S(2)}) collective-permute-start(bf16[128,768]{1,0:T(8,128)(2,1)S(1)} %slice.9), channel_id=1, source_target_pairs={{0,7},{1,0},{2,1},{3,2},{4,3},{5,4},{6,5},{7,6},{8,15},{9,8},{10,9... | collective-permute-start | bytes 589832 | tf_op jit(solution)/shard_map/ppermute | solution.py:28
  90.0 0.9 copy-start.10
  93.5 1.4 copy-start
  142.9 10.2 %copy-start.7 = (f32[1,1024]{1,0:T(1,128)S(1)}, f32[1,1024]{1,0:T(1,128)}, u32[]{:S(2)}) copy-start(f32[1,1024]{1,0:T(1,128)} %get-tuple-element.29) | copy-start | bytes 12292
  142.9 11.9 %copy-start.9 = (f32[1,16]{1,0:T(1,128)S(1)}, f32[1,16]{1,0:T(1,128)}, u32[]{:S(2)}) copy-start(f32[1,16]{1,0:T(1,128)} %param.18) | copy-start | bytes 196
  145.1 37.4 %all-to-all-start.2 = ((bf16[64,4,2176]{2,1,0:T(4,128)(2,1)}), bf16[64,4,2176]{2,1,0:T(4,128)(2,1)S(1)}, u32[]{:S(2)}, u32[]{:S(2)}) async-start(bf16[64,4,2176]{2,1,0:T(4,128)(2,1)} %reshape.75), calls=%async_computation.2 | async-start | bytes 2228224 | tf_op jit(solution)/shard_map/all_to_all | solution.py:23
  (1 other events, 0.7 us)
Sparse Core Ops, SparseCore 0:
  10.7 70.4 all-gather.4
  83.2 46.7 all-gather.6
  134.2 44.3 reduce-scatter.1

commit v5 on v4

--- a/solution.py
+++ b/solution.py
@@ -35,7 +35,7 @@
         in_specs=in_specs,
         out_specs=jax.tree.map(lambda _: VMEM, out_shape),
         cost_estimate=pl.CostEstimate(flops=flops, bytes_accessed=moved, transcendentals=0),
-        compiler_params=pltpu.CompilerParams(vmem_limit_bytes=60 * 1024 * 1024),
+        compiler_params=pltpu.CompilerParams(vmem_limit_bytes=32 * 1024 * 1024),
     )
 
 

time: 194 us -> 205 us (1.057)
  local copies, waits for them, and re-layouts: 7.82 us -> 41.3 us
  Pallas kernels: 33.3 us -> 16.5 us
  waiting for transfers between devices: 61.6 us -> 58.5 us
  blocking collectives: 24.1 us -> 21.5 us
    unnamed x25 -> x101, local copies, waits for them, and re-layouts: 2.89 us -> 37.8 us
    ppermute x8, waiting for transfers between devices: 33.5 us -> 27 us  [shift(): lax.ppermute(block, 'replica', [(i, (i + step) % count) for i in range(co...]
    pallas_call x1, Pallas kernels: 8.76 us -> 4.87 us  [local(): call(functools.partial(backward_body, replicas), [shape((slots, width + L...]
    all_to_all x2, waiting for transfers between devices: 27.3 us -> 30.7 us  [exchange(): lax.all_to_all(rows, 'expert', split_axis=0, concat_axis=0, tiled=True)]
    pallas_call x1, Pallas kernels: 4.51 us -> 1.33 us  [local(): call(functools.partial(partial_body, capacity), [shape((slots, width), BF...]
    pallas_call x1, Pallas kernels: 4.12 us -> 1.44 us  [local(): call(functools.partial(pack_body, experts, capacity), [shape((2 * slots,...]
    pallas_call x1, Pallas kernels: 8.82 us -> 6.18 us  [local(): call(functools.partial(forward_body, replicas, capacity), [shape((slots,...]
    all_to_all x1, blocking collectives: 24.1 us -> 21.5 us  [exchange(): lax.all_to_all(rows, 'expert', split_axis=0, concat_axis=0, tiled=True)]
  transfers between devices with their start and end apart: 13 -> 13, of which waited for: 5 -> 6; matrix products, arithmetic and copies ran while one was open for 5% -> 3% of each run, Pallas kernels for 14% -> 7%
where the time goes in v5:
time: 205 us; the launch traced here: 203 us
  waiting for transfers between devices  58.5 us (29%)
  starting transfers between devices  48 us (23%)
  local copies, waits for them, and re-layouts  41.3 us (20%)
  blocking collectives  21.5 us (10%)
  Pallas kernels  16.5 us (8%)
  between operations  14.1 us (7%)
  other arithmetic  3.49 us (2%)
    unnamed x101, local copies, waits for them, and re-layouts  37.8 us
    all_to_all x2, waiting for transfers between devices, exchange(): lax.all_to_all(rows, 'expert', split_axis=0, concat_axis=0, tiled=True)  30.7 us
    ppermute x8, starting transfers between devices, shift(): lax.ppermute(block, 'replica', [(i, (i + step) % count) for i in range(co...  27.3 us
    ppermute x8, waiting for transfers between devices, shift(): lax.ppermute(block, 'replica', [(i, (i + step) % count) for i in range(co...  27 us
    all_to_all x1, blocking collectives, exchange(): lax.all_to_all(rows, 'expert', split_axis=0, concat_axis=0, tiled=True)  21.5 us
    all_to_all x2, starting transfers between devices, exchange(): lax.all_to_all(rows, 'expert', split_axis=0, concat_axis=0, tiled=True)  20.6 us
    pallas_call x1, Pallas kernels, local(): call(functools.partial(forward_body, replicas, capacity), [shape((slots,...  6.18 us
    pallas_call x1, Pallas kernels, local(): call(functools.partial(backward_body, replicas), [shape((slots, width + L...  4.87 us
  transfers between devices with their start and end apart: 13, of which 6 were waited for; matrix products, arithmetic and copies ran while one was open for 3% of the time, Pallas kernels for 7%

profile of v5, /device:TPU:1, one launch (start us, length us, event | category | flops | bytes accessed | tf_op | source)
XLA Modules:
  0.0 203.3 jit_solution(5392790805334432018)
XLA Ops:
  11.8 4.0 %collective-permute-start = (bf16[256,768]{1,0:T(8,128)(2,1)}, bf16[256,768]{1,0:T(8,128)(2,1)S(1)}, u32[]{:S(2)}, u32[]{:S(2)}) collective-permute-start(bf16[256,768]{1,0:T(8,128)(2,1)} %bitcast.31), channel_id=1, source_target_pairs={{0,1},{1,2},{2,3},{3,4},{4,5},{5,6},{6,7},{7,0},{8,9},{9,10},{10,1... | collective-permute-start | bytes 1179656 | tf_op jit(solution)/shard_map/ppermute | solution.py:28
  15.9 3.8 %collective-permute-start.1 = (bf16[256,768]{1,0:T(8,128)(2,1)}, bf16[256,768]{1,0:T(8,128)(2,1)S(1)}, u32[]{:S(2)}, u32[]{:S(2)}) collective-permute-start(bf16[256,768]{1,0:T(8,128)(2,1)} %bitcast.32), channel_id=1, source_target_pairs={{0,7},{1,0},{2,1},{3,2},{4,3},{5,4},{6,5},{7,6},{8,15},{9,8},{10,9... | collective-permute-start | bytes 1179656 | tf_op jit(solution)/shard_map/ppermute | solution.py:28
  23.8 1.4 shard_map.129
  25.2 1.4 copy-done.8
  26.7 14.4 %all-to-all-start = ((bf16[64,8,2176]{2,1,0:T(8,128)(2,1)}), bf16[64,8,2176]{2,1,0:T(8,128)(2,1)S(1)}, u32[]{:S(2)}, u32[]{:S(2)}) async-start(bf16[64,8,2176]{2,1,0:T(8,128)(2,1)} %bitcast.30), calls=%async_computation | async-start | bytes 4456448 | tf_op jit(solution)/shard_map/all_to_all | solution.py:23
  41.1 1.9 collective-permute-start.2
  43.8 4.6 %collective-permute-start.3 = (bf16[256,768]{1,0:T(8,128)(2,1)S(1)}, bf16[256,768]{1,0:T(8,128)(2,1)}, u32[]{:S(2)}, u32[]{:S(2)}) collective-permute-start(bf16[256,768]{1,0:T(8,128)(2,1)S(1)} %collective-permute-done.1.rest_2_), channel_id=1, source_target_pairs={{0,7},{1,0},{2,1},{3,2},{4,3},{5,4},{6,5},{7,6},{8,15},{9,8},{10,9... | collective-permute-start | bytes 1179656 | tf_op jit(solution)/shard_map/ppermute | solution.py:28
  49.1 14.4 %collective-permute-done.2.rest_3_ = bf16[256,768]{1,0:T(8,128)(2,1)} collective-permute-done((bf16[256,768]{1,0:T(8,128)(2,1)S(1)}, bf16[256,768]{1,0:T(8,128)(2,1)}, u32[]{:S(2)}, u32[]{:S(2)}) %collective-permute-start.2) | collective-permute-done | bytes 393248 | tf_op jit(solution)/shard_map/ppermute | solution.py:28
  63.6 1.9 collective-permute-start.4
  65.5 4.6 %collective-permute-start.5 = (bf16[256,768]{1,0:T(8,128)(2,1)}, bf16[256,768]{1,0:T(8,128)(2,1)S(1)}, u32[]{:S(2)}, u32[]{:S(2)}) collective-permute-start(bf16[256,768]{1,0:T(8,128)(2,1)} %collective-permute-done.3.rest_4_), channel_id=1, source_target_pairs={{0,7},{1,0},{2,1},{3,2},{4,3},{5,4},{6,5},{7,6},{8,15},{9,8},{10,9... | collective-permute-start | bytes 1179656 | tf_op jit(solution)/shard_map/ppermute | solution.py:28
  71.0 10.8 %collective-permute-done.4.rest_5_ = bf16[256,768]{1,0:T(8,128)(2,1)S(1)} collective-permute-done((bf16[256,768]{1,0:T(8,128)(2,1)}, bf16[256,768]{1,0:T(8,128)(2,1)S(1)}, u32[]{:S(2)}, u32[]{:S(2)}) %collective-permute-start.4) | collective-permute-done | bytes 393248 | tf_op jit(solution)/shard_map/ppermute | solution.py:28
  81.8 1.9 collective-permute-start.6
  83.8 4.6 %collective-permute-start.7 = (bf16[128,768]{1,0:T(8,128)(2,1)S(1)}, bf16[128,768]{1,0:T(8,128)(2,1)S(1)}, u32[]{:S(2)}, u32[]{:S(2)}) collective-permute-start(bf16[128,768]{1,0:T(8,128)(2,1)S(1)} %slice.9), channel_id=1, source_target_pairs={{0,7},{1,0},{2,1},{3,2},{4,3},{5,4},{6,5},{7,6},{8,15},{9,8},{10,9... | collective-permute-start | bytes 589832 | tf_op jit(solution)/shard_map/ppermute | solution.py:28
  92.1 2.8 %all-to-all-done = bf16[64,8,2176]{2,1,0:T(8,128)(2,1)S(1)} async-done(((bf16[64,8,2176]{2,1,0:T(8,128)(2,1)}), bf16[64,8,2176]{2,1,0:T(8,128)(2,1)S(1)}, u32[]{:S(2)}, u32[]{:S(2)}) %all-to-all-start) | async-done | bytes 2228256 | tf_op jit(solution)/shard_map/all_to_all | solution.py:23
  94.9 2.0 %copy-done = bf16[2176,768]{1,0:T(8,128)(2,1)S(1)} copy-done((bf16[2176,768]{1,0:T(8,128)(2,1)S(1)}, bf16[2176,768]{1,0:T(8,128)(2,1)}, u32[]{:S(2)}) %copy-start) | copy-done | bytes 3342360
  100.0 6.2 %shard_map.132 = (bf16[256,2048]{1,0:T(8,128)(2,1)S(1)}, bf16[256,768]{1,0:T(8,128)(2,1)S(1)}, bf16[256,768]{1,0:T(8,128)(2,1)S(1)}, bf16[256,768]{1,0:T(8,128)(...) custom-call(s32[1]{0:T(128)} %bitcast.me, bf16[512,2176]{1,0:T(8,128)(2,1)S(1)} %bitcast.28, ...), custom_call_target="tpu_custom_call" | custom-call | flops 1610612736 | bytes 6291456 | tf_op jit(solution)/shard_map/pallas_call | solution.py:272
  109.7 21.5 %all_to_all.18 = f32[64,1,1024]{2,1,0:T(1,128)S(1)} all-to-all(f32[64,1,1024]{2,1,0:T(1,128)S(1)} %broadcast_in_dim.58), channel_id=1, replica_groups=mesh['expert'=64,'replica'=8] {'expert'}, dimensions={0} | all-to-all | bytes 524288 | tf_op jit(solution)/shard_map/all_to_all | solution.py:23
  134.8 1.7 copy-done.2
  137.5 1.9 copy-done.3
  149.7 4.9 %shard_map.134 = (bf16[256,2176]{1,0:T(8,128)(2,1)S(1)}, bf16[256,768]{1,0:T(8,128)(2,1)}, bf16[256,768]{1,0:T(8,128)(2,1)}) custom-call(s32[1]{0:T(128)} %bitcast.me, bf16[256,2048]{1,0:T(8,128)(2,1)S(1)} %copy-done.27, bf16[768,2048]{1,0:T(8,128)(2,1)S(1)} %bitcast.29, bf16[256,768]{1,0:T(8,128)(2,1)S(1)} %copy-done.29, bf16[256,768]{1,0:T(8,128)(2,1)S(1)} %copy-done.31, ...), custom_call_target="tpu_custom_call" | custom-call | flops 2415919104 | bytes 9437184 | tf_op jit(solution)/shard_map/pallas_call | solution.py:313
  155.6 2.2 %reshape.75 = bf16[64,4,2176]{2,1,0:T(4,128)(2,1)} reshape(bf16[256,2176]{1,0:T(8,128)(2,1)} %copy-done.25) | data formatting | bytes 2228224 | tf_op jit(solution)/shard_map/reshape | solution.py:324
  157.8 6.2 %all-to-all-start.2 = ((bf16[64,4,2176]{2,1,0:T(4,128)(2,1)}), bf16[64,4,2176]{2,1,0:T(4,128)(2,1)S(1)}, u32[]{:S(2)}, u32[]{:S(2)}) async-start(bf16[64,4,2176]{2,1,0:T(4,128)(2,1)} %reshape.75), calls=%async_computation.2 | async-start | bytes 2228224 | tf_op jit(solution)/shard_map/all_to_all | solution.py:23
  166.1 27.9 %all-to-all-done.2 = bf16[64,4,2176]{2,1,0:T(4,128)(2,1)S(1)} async-done(((bf16[64,4,2176]{2,1,0:T(4,128)(2,1)}), bf16[64,4,2176]{2,1,0:T(4,128)(2,1)S(1)}, u32[]{:S(2)}, u32[]{:S(2)}) %all-to-all-start.2) | async-done | bytes 1114144 | tf_op jit(solution)/shard_map/all_to_all | solution.py:23
  195.3 1.4 shard_map.135
  (132 shorter events, 40.6 us)
Async XLA Ops:
  7.2 87.8 %all-gather.5.cloned.1.call-start = ((), (), s32[]{:S(2)}) async-start(), calls=%async_computation.5 | async-start | bytes 3760128 | tf_op jit(solution)/shard_map/all_gather | solution.py:245
  11.1 126.4 %all-gather.7.cloned.1.call-start = ((), (), s32[]{:S(2)}) async-start(), calls=%async_computation.6 | async-start | bytes 3538944 | tf_op jit(solution)/shard_map/all_gather | solution.py:287
  11.8 29.3 %collective-permute-start = (bf16[256,768]{1,0:T(8,128)(2,1)}, bf16[256,768]{1,0:T(8,128)(2,1)S(1)}, u32[]{:S(2)}, u32[]{:S(2)}) collective-permute-start(bf16[256,768]{1,0:T(8,128)(2,1)} %bitcast.31), channel_id=1, source_target_pairs={{0,1},{1,2},{2,3},{3,4},{4,5},{5,6},{6,7},{7,0},{8,9},{9,10},{10,1... | collective-permute-start | bytes 1179656 | tf_op jit(solution)/shard_map/ppermute | solution.py:28
  15.9 27.9 %collective-permute-start.1 = (bf16[256,768]{1,0:T(8,128)(2,1)}, bf16[256,768]{1,0:T(8,128)(2,1)S(1)}, u32[]{:S(2)}, u32[]{:S(2)}) collective-permute-start(bf16[256,768]{1,0:T(8,128)(2,1)} %bitcast.32), channel_id=1, source_target_pairs={{0,7},{1,0},{2,1},{3,2},{4,3},{5,4},{6,5},{7,6},{8,15},{9,8},{10,9... | collective-permute-start | bytes 1179656 | tf_op jit(solution)/shard_map/ppermute | solution.py:28
  26.6 44.0 %copy-start.10 = (bf16[128,2048]{1,0:T(8,128)(2,1)S(1)}, bf16[128,2048]{1,0:T(8,128)(2,1)}, u32[]{:S(2)}) copy-start(bf16[128,2048]{1,0:T(8,128)(2,1)} %tokens.1) | copy-start | bytes 1572868
  26.6 44.0 %copy-start.38 = (f32[2048]{0:T(1024)S(1)}, f32[2048]{0:T(1024)}, u32[]{:S(2)}) copy-start(f32[2048]{0:T(1024)} %param.14) | copy-start | bytes 24580
  26.6 44.2 %copy-start.40 = (s32[1,128]{1,0:T(1,128)S(1)}, s32[1,128]{1,0:T(1,128)}, u32[]{:S(2)}) copy-start(s32[1,128]{1,0:T(1,128)} %nodes.1) | copy-start | bytes 1540
  26.7 68.3 %all-to-all-start = ((bf16[64,8,2176]{2,1,0:T(8,128)(2,1)}), bf16[64,8,2176]{2,1,0:T(8,128)(2,1)S(1)}, u32[]{:S(2)}, u32[]{:S(2)}) async-start(bf16[64,8,2176]{2,1,0:T(8,128)(2,1)} %bitcast.30), calls=%async_computation | async-start | bytes 4456448 | tf_op jit(solution)/shard_map/all_to_all | solution.py:23
  41.1 153.2 %reduce-scatter.2.cloned.1.call-start = ((), (), s32[]{:S(2)}) async-start(), calls=%async_computation.4 | async-start | bytes 3538944 | tf_op jit(solution)/shard_map/reduce_scatter | solution.py:311
  41.1 22.4 %collective-permute-start.2 = (bf16[256,768]{1,0:T(8,128)(2,1)S(1)}, bf16[256,768]{1,0:T(8,128)(2,1)}, u32[]{:S(2)}, u32[]{:S(2)}) collective-permute-start(bf16[256,768]{1,0:T(8,128)(2,1)S(1)} %collective-permute-done.rest_1_), channel_id=1, source_target_pairs={{0,1},{1,2},{2,3},{3,4},{4,5},{5,6},{6,7},{7,0},{8,9},{9,10},{10,1... | collective-permute-start | bytes 1179656 | tf_op jit(solution)/shard_map/ppermute | solution.py:28
  43.8 21.7 %collective-permute-start.3 = (bf16[256,768]{1,0:T(8,128)(2,1)S(1)}, bf16[256,768]{1,0:T(8,128)(2,1)}, u32[]{:S(2)}, u32[]{:S(2)}) collective-permute-start(bf16[256,768]{1,0:T(8,128)(2,1)S(1)} %collective-permute-done.1.rest_2_), channel_id=1, source_target_pairs={{0,7},{1,0},{2,1},{3,2},{4,3},{5,4},{6,5},{7,6},{8,15},{9,8},{10,9... | collective-permute-start | bytes 1179656 | tf_op jit(solution)/shard_map/ppermute | solution.py:28
  63.6 18.2 %collective-permute-start.4 = (bf16[256,768]{1,0:T(8,128)(2,1)}, bf16[256,768]{1,0:T(8,128)(2,1)S(1)}, u32[]{:S(2)}, u32[]{:S(2)}) collective-permute-start(bf16[256,768]{1,0:T(8,128)(2,1)} %collective-permute-done.2.rest_3_), channel_id=1, source_target_pairs={{0,1},{1,2},{2,3},{3,4},{4,5},{5,6},{6,7},{7,0},{8,9},{9,10},{10,1... | collective-permute-start | bytes 1179656 | tf_op jit(solution)/shard_map/ppermute | solution.py:28
  65.5 18.3 %collective-permute-start.5 = (bf16[256,768]{1,0:T(8,128)(2,1)}, bf16[256,768]{1,0:T(8,128)(2,1)S(1)}, u32[]{:S(2)}, u32[]{:S(2)}) collective-permute-start(bf16[256,768]{1,0:T(8,128)(2,1)} %collective-permute-done.3.rest_4_), channel_id=1, source_target_pairs={{0,7},{1,0},{2,1},{3,2},{4,3},{5,4},{6,5},{7,6},{8,15},{9,8},{10,9... | collective-permute-start | bytes 1179656 | tf_op jit(solution)/shard_map/ppermute | solution.py:28
  81.8 13.1 %copy-start.4 = (bf16[256,768]{1,0:T(8,128)(2,1)}, bf16[256,768]{1,0:T(8,128)(2,1)S(1)}, u32[]{:S(2)}) copy-start(bf16[256,768]{1,0:T(8,128)(2,1)S(1)} %collective-permute-done.4.rest_5_) | copy-start | bytes 1179652
  81.8 8.5 %collective-permute-start.6 = (bf16[128,768]{1,0:T(8,128)(2,1)S(1)}, bf16[128,768]{1,0:T(8,128)(2,1)S(1)}, u32[]{:S(2)}, u32[]{:S(2)}) collective-permute-start(bf16[128,768]{1,0:T(8,128)(2,1)S(1)} %slice.8), channel_id=1, source_target_pairs={{0,1},{1,2},{2,3},{3,4},{4,5},{5,6},{6,7},{7,0},{8,9},{9,10},{10,1... | collective-permute-start | bytes 589832 | tf_op jit(solution)/shard_map/ppermute | solution.py:28
  83.8 11.1 %copy-start.6 = (bf16[256,768]{1,0:T(8,128)(2,1)}, bf16[256,768]{1,0:T(8,128)(2,1)S(1)}, u32[]{:S(2)}) copy-start(bf16[256,768]{1,0:T(8,128)(2,1)S(1)} %collective-permute-done.5.rest_6_) | copy-start | bytes 1179652
  83.8 7.5 %collective-permute-start.7 = (bf16[128,768]{1,0:T(8,128)(2,1)S(1)}, bf16[128,768]{1,0:T(8,128)(2,1)S(1)}, u32[]{:S(2)}, u32[]{:S(2)}) collective-permute-start(bf16[128,768]{1,0:T(8,128)(2,1)S(1)} %slice.9), channel_id=1, source_target_pairs={{0,7},{1,0},{2,1},{3,2},{4,3},{5,4},{6,5},{7,6},{8,15},{9,8},{10,9... | collective-permute-start | bytes 589832 | tf_op jit(solution)/shard_map/ppermute | solution.py:28
  100.0 9.4 %copy-start.46 = (pred[64]{0:T(512)(128)(4,1)S(1)}, pred[64]{0:T(512)(128)(4,1)}, u32[]{:S(2)}) copy-start(pred[64]{0:T(512)(128)(4,1)} %iota_compare_fusion.1) | copy-start | bytes 196
  100.0 9.4 %copy-start.48 = (f32[16]{0:T(128)S(1)}, f32[16]{0:T(128)}, u32[]{:S(2)}) copy-start(f32[16]{0:T(128)} %fusion) | copy-start | bytes 196
  155.6 9.7 %copy-start.47 = (pred[64]{0:T(512)(128)(4,1)S(1)}, pred[64]{0:T(512)(128)(4,1)}, u32[]{:S(2)}) copy-start(pred[64]{0:T(512)(128)(4,1)} %iota_compare_fusion.1) | copy-start | bytes 196
  155.6 10.0 %copy-start.49 = (f32[1,16]{1,0:T(1,128)S(1)}, f32[1,16]{1,0:T(1,128)}, u32[]{:S(2)}) copy-start(f32[1,16]{1,0:T(1,128)} %param.18) | copy-start | bytes 196
  157.8 36.5 %copy-start.12 = (bf16[128,2048]{1,0:T(8,128)(2,1)S(1)}, bf16[128,2048]{1,0:T(8,128)(2,1)}, u32[]{:S(2)}) copy-start(bf16[128,2048]{1,0:T(8,128)(2,1)} %above.3) | copy-start | bytes 1572868
  157.8 36.5 %copy-start.42 = (f32[128,1]{0,1:T(1,128)S(1)}, f32[128,1]{0,1:T(1,128)}, u32[]{:S(2)}) copy-start(f32[128,1]{0,1:T(1,128)} %param.16) | copy-start | bytes 1540
  157.8 36.2 %all-to-all-start.2 = ((bf16[64,4,2176]{2,1,0:T(4,128)(2,1)}), bf16[64,4,2176]{2,1,0:T(4,128)(2,1)S(1)}, u32[]{:S(2)}, u32[]{:S(2)}) async-start(bf16[64,4,2176]{2,1,0:T(4,128)(2,1)} %reshape.75), calls=%async_computation.2 | async-start | bytes 2228224 | tf_op jit(solution)/shard_map/all_to_all | solution.py:23
  (39 other events, 47.2 us)
Sparse Core Ops, SparseCore 0:
  11.2 66.6 all-gather.4
  80.0 48.1 all-gather.6
  137.6 41.8 reduce-scatter.1
